TPU v7x, 256 devices: a whole 4x4x8 slice. The times are simulated.
256 devices in a mesh: ta: 4 (over z_lo), gx: 8 (over y, z_hi), gy: 8 (over x, core).
Axes of the slice: x: 4, y: 4, z: 8 (z_hi: 2, z_lo: 4; z = z_hi * 4 + z_lo), core: 2. Of those that a mesh axis runs over, the one named last changes fastest.
Arguments:
- momenta: float32 [3, 128, 512, 1024], P(None, 'ta', 'gx', 'gy'), may hold values from -3 to 4.1, as said below
- potential: float32 [128, 512, 1024], P('ta', 'gx', 'gy'), may hold values from -6 to 6
- rho_start: float32 [512, 1024], P('gx', 'gy'), may hold values from 0.25 to 4
- rho_end: float32 [512, 1024], P('gx', 'gy'), may hold values from 0.25 to 4
Outputs:
- updated_momenta: float32 [3, 128, 512, 1024], P(None, 'ta', 'gx', 'gy')
- updated_potential: float32 [128, 512, 1024], P('ta', 'gx', 'gy')
Inputs may be any that keep to these rules, and one draw needn't show every extreme that they name: `momenta`: component 0 (density) is positive, between 0.22 and 4.1; components 1 and 2 lie between -3 and 3.
All inputs are finite; a program needn't handle non-finite values.
Results may differ from a plain program's by a relative error of at most 0.0007.
Values sent between devices are 32-bit elements; how exact they have to be, the bound alone decides.
A program may use at most 128 MiB of HBM per device.

v0:
```python
import jax
import jax.numpy as jnp
from jax import lax
from jax.sharding import PartitionSpec as P

NT = 128
NX = 512
NY = 1024
ITERS = 2
NEWTON = 8


penalty = 1.0
highest = lax.Precision.HIGHEST


def padded_2(array, sides, width):
    for axis, dim in sides:
        size, length = (lax.axis_size(axis), array.shape[dim])
        up = [(i, (i + 1) % size) for i in range(size - 1)]
        down = [(j, i) for i, j in up]
        last = lax.slice_in_dim(array, length - width, length, axis=dim)
        first = lax.slice_in_dim(array, 0, width, axis=dim)
        before = lax.ppermute(last, axis, up)
        after = lax.ppermute(first, axis, down)
        array = jnp.concatenate([before, array, after], axis=dim)
    return array


def cosine_table(count):
    modes = jnp.arange(count, dtype=jnp.int32)[:, None]
    cells = jnp.arange(count, dtype=jnp.int32)[None, :]
    phase = modes * (2 * cells + 1) % (4 * count)
    angle = phase.astype(jnp.float32) * (jnp.pi / (2 * count))
    weight = jnp.where(modes == 0, 1.0, 2.0).astype(jnp.float32) / count
    return jnp.sqrt(weight) * jnp.cos(angle)


def eigenvalue(modes, count):
    half_angle = modes.astype(jnp.float32) * (jnp.pi / (2 * count))
    return (2.0 * jnp.sin(half_angle)) ** 2


def multiplier(time_modes, x_modes, y_modes):
    spectrum = (
        eigenvalue(time_modes, NT)[:, None, None]
        + eigenvalue(x_modes, NX)[None, :, None]
        + eigenvalue(y_modes, NY)[None, None, :]
    )
    anchor = (
        (time_modes[:, None, None] == 0)
        & (x_modes[None, :, None] == 0)
        & (y_modes[None, None, :] == 0)
    ).astype(jnp.float32)
    return (1.0 - anchor) / (penalty * (spectrum + anchor))


def project(lifted):
    along_time, along_x, along_y = (lifted[0], lifted[1], lifted[2])
    squares = along_x * along_x + along_y * along_y
    shift_value = jnp.zeros_like(along_time)
    for newton_index in range(NEWTON):
        growth = 1.0 + shift_value
        residual = along_time - shift_value + squares / (2.0 * growth * growth)
        slope = -1.0 - squares / (growth * growth * growth)
        shift_value = jnp.maximum(shift_value - residual / slope, 0.0)
    growth = 1.0 + shift_value
    return jnp.stack([along_time - shift_value, along_x / growth, along_y / growth])


def exchange_y(blocked):
    return lax.all_to_all(blocked, "gy", split_axis=0, concat_axis=0, tiled=True)


def exchange_x(blocked):
    return lax.all_to_all(blocked, "gx", split_axis=0, concat_axis=0, tiled=True)


def exchange_time_y(blocked):
    return lax.all_to_all(blocked, ("ta", "gy"), split_axis=0, concat_axis=0, tiled=True)


def face_layers(stacked):
    return padded_2(stacked, (("ta", 1), ("gx", 2), ("gy", 3)), 1)


def on_device(momenta, potential, rho_start, rho_end):
    count_ta = lax.axis_size("ta")
    count_gx = lax.axis_size("gx")
    count_gy = lax.axis_size("gy")
    index_ta = lax.axis_index("ta")
    index_gx = lax.axis_index("gx")
    index_gy = lax.axis_index("gy")
    span_t, span_x, span_y = potential.shape
    time_cells = index_ta * span_t + jnp.arange(span_t, dtype=jnp.int32)
    x_cells = index_gx * span_x + jnp.arange(span_x, dtype=jnp.int32)
    y_cells = index_gy * span_y + jnp.arange(span_y, dtype=jnp.int32)
    keep_time = (time_cells < NT - 1).astype(jnp.float32)[:, None, None]
    keep_x = (x_cells < NX - 1).astype(jnp.float32)[None, :, None]
    keep_y = (y_cells < NY - 1).astype(jnp.float32)[None, None, :]
    first_plane = (time_cells == 0).astype(jnp.float32)[:, None, None]
    last_plane = (time_cells == NT - 1).astype(jnp.float32)[:, None, None]
    boundary = last_plane * rho_end[None] - first_plane * rho_start[None]
    table_time = cosine_table(NT)
    table_x = cosine_table(NX)
    table_y = cosine_table(NY)
    group_size = count_ta * count_gy
    sub_time = span_t // count_gy
    wide_y = NY // count_gx
    narrow_x = NX // group_size
    blocks_y = table_y.reshape(count_gx, wide_y, count_gy, span_y)
    blocks_x = table_x.reshape(group_size, narrow_x, count_gx, span_x)
    blocks_time = table_time.reshape(NT, group_size, sub_time)
    own_group = index_ta * count_gy + index_gy
    spectral_scale = multiplier(
        jnp.arange(NT, dtype=jnp.int32),
        own_group * narrow_x + jnp.arange(narrow_x, dtype=jnp.int32),
        index_gx * wide_y + jnp.arange(wide_y, dtype=jnp.int32),
    )
    for sweep_index in range(ITERS):
        padded = face_layers(potential[None])
        slopes = jnp.stack(
            [
                (padded[0, 2:, 1:-1, 1:-1] - potential) * keep_time,
                (padded[0, 1:-1, 2:, 1:-1] - potential) * keep_x,
                (padded[0, 1:-1, 1:-1, 2:] - potential) * keep_y,
            ]
        )
        lifted = slopes + momenta / penalty
        cone = project(lifted)
        momenta = momenta + penalty * (slopes - cone)
        flows = momenta - penalty * cone
        masked = jnp.stack([flows[0] * keep_time, flows[1] * keep_x, flows[2] * keep_y])
        padded = face_layers(masked)
        source = (
            masked[0]
            - padded[0, :-2, 1:-1, 1:-1]
            + (masked[1] - padded[1, 1:-1, :-2, 1:-1])
            + (masked[2] - padded[2, 1:-1, 1:-1, :-2])
            + boundary
        )
        blocked = exchange_y(source.reshape(count_gy, sub_time, span_x, span_y))
        blocked = jnp.einsum("suxj,bksj->buxk", blocked, blocks_y, precision=highest)
        blocked = exchange_x(blocked)
        blocked = jnp.einsum("suxk,cqsx->cuqk", blocked, blocks_x, precision=highest)
        blocked = exchange_time_y(blocked)
        spectral = (
            jnp.einsum("suqk,wsu->wqk", blocked, blocks_time, precision=highest) * spectral_scale
        )
        blocked = exchange_time_y(
            jnp.einsum("wqk,wsu->suqk", spectral, blocks_time, precision=highest)
        )
        blocked = exchange_x(jnp.einsum("cuqk,cqsx->suxk", blocked, blocks_x, precision=highest))
        blocked = exchange_y(jnp.einsum("buxk,bksj->suxj", blocked, blocks_y, precision=highest))
        potential = blocked.reshape(span_t, span_x, span_y)
    return (momenta, potential)


def solution(mesh):
    placed = (P(None, "ta", "gx", "gy"), P("ta", "gx", "gy"), P("gx", "gy"), P("gx", "gy"))
    return jax.shard_map(
        on_device,
        mesh=mesh,
        in_specs=placed,
        out_specs=(P(None, "ta", "gx", "gy"), P("ta", "gx", "gy")),
        check_vma=False,
    )
```

profile of v0, /device:TPU:1, one launch (start us, length us, event | category | flops | bytes accessed | tf_op | source)
XLA Modules:
  0.0 663.7 jit_solution(9288176385095457379)
XLA Ops:
  2.8 5.0 collective-permute-start.1
  11.1 9.3 %collective-permute-start.3 = (f32[1,34,1,128]{3,2,1,0:T(1,128)S(1)}, f32[1,34,1,128]{3,2,1,0:T(1,128)S(1)}, u32[]{:S(2)}, u32[]{:S(2)}) collective-permute-start(f32[1,34,1,128]{3,2,1,0:T(1,128)S(1)} %get-tuple-element.49), channel_id=1, source_target_pairs={{0,8},{8,16},{16,24},{24,32},{32,40},{40,48},{48,56},{1,9},{9,17},... | collective-permute-start | bytes 52232 | tf_op jit(solution)/shard_map/ppermute | solution.py:24
  21.2 1.3 pad_maximum_fusion.20
  23.0 5.0 collective-permute-start.4
  28.1 2.0 collective-permute-done.4
  33.6 4.5 slice_subtract_fusion.1
  38.4 1.4 fusion.15
  39.8 1.8 fusion.263
  42.9 4.6 collective-permute-start.5
  47.9 1.8 collective-permute-done.5
  49.7 8.0 %collective-permute-start.7 = (f32[3,34,1,128]{3,2,1,0:T(1,128)S(1)}, f32[3,34,1,128]{3,2,1,0:T(1,128)S(1)}, u32[]{:S(2)}, u32[]{:S(2)}) collective-permute-start(f32[3,34,1,128]{3,2,1,0:T(1,128)S(1)} %get-tuple-element.22), channel_id=1, source_target_pairs={{0,8},{8,16},{16,24},{24,32},{32,40},{40,48},{48,56},{1,9},{9,17},... | collective-permute-start | bytes 156680 | tf_op jit(solution)/shard_map/ppermute | solution.py:24
  59.3 9.4 %collective-permute-done.8 = f32[3,34,1,128]{3,2,1,0:T(1,128)S(1)} collective-permute-done((f32[3,34,1,128]{3,2,1,0:T(1,128)S(1)}, f32[3,34,1,128]{3,2,1,0:T(1,128)S(1)}, u32[]{:S(2)}, u32[]{:S(2)}) %collective-permute-start.8) | collective-permute-done | bytes 52256 | tf_op jit(solution)/shard_map/ppermute | solution.py:25
  68.8 4.8 pad_maximum_fusion.6
  73.6 3.7 copy.52
  77.3 3.7 collective-permute-start.9
  82.3 3.6 copy.53
  85.9 3.0 pad_maximum_fusion.41
  89.0 2.1 fusion.196
  91.2 6.1 all-to-all-start
  97.3 15.1 %all-to-all-done = f32[8,4,64,128]{3,2,1,0:T(8,128)} async-done(((f32[8,4,64,128]{3,2,1,0:T(8,128)}), f32[8,4,64,128]{3,2,1,0:T(8,128)}, u32[]{:S(2)}, u32[]{:S(2)}) %all-to-all-start) | async-done | bytes 1048608 | tf_op jit(solution)/shard_map/all_to_all | solution.py:72
  112.4 21.5 %fusion.45 = f32[8,4,64,128]{3,2,1,0:T(8,128)} fusion(f32[8,4,64,128]{3,2,1,0:T(8,128)} %all-to-all-done, s32[8,128]{1,0:T(8,128)S(1)} %get-tuple-element.58, s32[8,128]{1,0:T(8,128)S(1)} %get-tuple-element.59, f32[8,128]{1,0:T(8,128)S(1)} %multiply_sqrt_fusion.1), kind=kOutput, calls=%fused_computation.97 | convolution fusion | flops 3236954112 | bytes 2109440 | tf_op jit(solution)/shard_map/suxj,bksj->buxk/dot_general | solution.py:143
  133.9 11.6 %all-to-all-start.1 = ((f32[8,4,64,128]{3,2,1,0:T(8,128)}), f32[8,4,64,128]{3,2,1,0:T(8,128)}, u32[]{:S(2)}, u32[]{:S(2)}) async-start(f32[8,4,64,128]{3,2,1,0:T(8,128)} %fusion.45), calls=%async_computation.1 | async-start | bytes 2097152 | tf_op jit(solution)/shard_map/all_to_all | solution.py:76
  145.6 18.4 %all-to-all-done.1 = f32[8,4,64,128]{3,2,1,0:T(8,128)} async-done(((f32[8,4,64,128]{3,2,1,0:T(8,128)}), f32[8,4,64,128]{3,2,1,0:T(8,128)}, u32[]{:S(2)}, u32[]{:S(2)}) %all-to-all-start.1) | async-done | bytes 1048608 | tf_op jit(solution)/shard_map/all_to_all | solution.py:76
  164.0 11.9 %fusion.33 = f32[32,4,16,128]{3,2,1,0:T(8,128)} fusion(f32[8,4,64,128]{3,2,1,0:T(8,128)} %all-to-all-done.1, s32[8,64]{1,0:T(8,128)S(1)} %multiply_add_fusion.1, s32[32,16]{1,0:T(8,128)S(1)} %multiply_add_fusion, f32[32,16]{1,0:T(8,128)S(1)} %multiply_sqrt_fusion), kind=kOutput, calls=%fused_computation.93 | convolution fusion | flops 1614544896 | bytes 2103296 | tf_op jit(solution)/shard_map/suxk,cqsx->cuqk/dot_general | solution.py:145
  175.9 17.8 %all-to-all-start.2 = ((f32[32,4,16,128]{3,2,1,0:T(8,128)}), f32[32,4,16,128]{3,2,1,0:T(8,128)}, u32[]{:S(2)}, u32[]{:S(2)}) async-start(f32[32,4,16,128]{3,2,1,0:T(8,128)} %fusion.33), calls=%async_computation.2 | async-start | bytes 2097152 | tf_op jit(solution)/shard_map/all_to_all | solution.py:80
  194.2 26.2 %all-to-all-done.2 = f32[32,4,16,128]{3,2,1,0:T(8,128)} async-done(((f32[32,4,16,128]{3,2,1,0:T(8,128)}), f32[32,4,16,128]{3,2,1,0:T(8,128)}, u32[]{:S(2)}, u32[]{:S(2)}) %all-to-all-start.2) | async-done | bytes 1048608 | tf_op jit(solution)/shard_map/all_to_all | solution.py:80
  220.4 3.2 fusion.58
  225.6 31.8 %all_to_all.60 = f32[32,4,16,128]{3,2,1,0:T(8,128)S(1)} all-to-all(f32[32,4,16,128]{3,2,1,0:T(8,128)S(1)} %copy.59), channel_id=1, replica_groups=mesh['ta'=4,'gx'=8,'gy'=8] {'ta','gy'}, dimensions={0} | all-to-all | bytes 2097152 | tf_op jit(solution)/shard_map/all_to_all | solution.py:80
  257.3 11.3 %fusion.39 = f32[8,4,64,128]{3,2,1,0:T(8,128)S(1)} fusion(f32[32,4,16,128]{3,2,1,0:T(8,128)S(1)} %all_to_all.60, s32[8,64]{1,0:T(8,128)S(1)} %multiply_add_fusion.1, s32[32,16]{1,0:T(8,128)S(1)} %multiply_add_fusion, f32[32,16]{1,0:T(8,128)S(1)} %multiply_sqrt_fusion), kind=kOutput, calls=%fused_computation.95 | convolution fusion | flops 1614544896 | bytes 2103296 | tf_op jit(solution)/shard_map/cuqk,cqsx->suxk/dot_general | solution.py:153
  268.7 24.5 %all_to_all.61 = f32[8,4,64,128]{3,2,1,0:T(8,128)S(1)} all-to-all(f32[8,4,64,128]{3,2,1,0:T(8,128)S(1)} %fusion.39), channel_id=1, replica_groups=mesh['ta'=4,'gx'=8,'gy'=8] {'gx'}, dimensions={0} | all-to-all | bytes 2097152 | tf_op jit(solution)/shard_map/all_to_all | solution.py:76
  293.1 19.8 %fusion.51 = f32[8,4,64,128]{3,2,1,0:T(8,128)S(1)} fusion(s32[8,128]{1,0:T(8,128)S(1)} %get-tuple-element.58, s32[8,128]{1,0:T(8,128)S(1)} %get-tuple-element.59, f32[8,128]{1,0:T(8,128)S(1)} %multiply_sqrt_fusion.1, f32[8,4,64,128]{3,2,1,0:T(8,128)S(1)} %all_to_all.61), kind=kOutput, calls=%fused_computation.101 | convolution fusion | flops 3236954112 | bytes 2109440 | tf_op jit(solution)/shard_map/buxk,bksj->suxj/dot_general | solution.py:154
  312.9 25.3 %all_to_all.62 = f32[8,4,64,128]{3,2,1,0:T(8,128)S(1)} all-to-all(f32[8,4,64,128]{3,2,1,0:T(8,128)S(1)} %fusion.51), channel_id=1, replica_groups=mesh['ta'=4,'gx'=8,'gy'=8] {'gy'}, dimensions={0} | all-to-all | bytes 2097152 | tf_op jit(solution)/shard_map/all_to_all | solution.py:72
  339.5 5.4 collective-permute-start.11
  347.2 7.9 %collective-permute-start.13 = (f32[1,34,1,128]{3,2,1,0:T(1,128)S(1)}, f32[1,34,1,128]{3,2,1,0:T(1,128)S(1)}, u32[]{:S(2)}, u32[]{:S(2)}) collective-permute-start(f32[1,34,1,128]{3,2,1,0:T(1,128)S(1)} %get-tuple-element.47), channel_id=1, source_target_pairs={{0,8},{8,16},{16,24},{24,32},{32,40},{40,48},{48,56},{1,9},{9,17},... | collective-permute-start | bytes 52232 | tf_op jit(solution)/shard_map/ppermute | solution.py:24
  357.2 1.7 copy.62
  358.9 4.9 collective-permute-start.14
  363.9 1.6 collective-permute-done.14
  365.4 1.5 copy.63
  367.0 3.9 fusion.163
  371.9 4.6 slice_subtract_fusion
  376.9 2.5 fusion.13
  379.4 1.8 fusion.262
  382.5 4.6 collective-permute-start.15
  388.0 1.7 collective-permute-done.15
  389.8 7.8 %collective-permute-start.17 = (f32[3,34,1,128]{3,2,1,0:T(1,128)S(1)}, f32[3,34,1,128]{3,2,1,0:T(1,128)S(1)}, u32[]{:S(2)}, u32[]{:S(2)}) collective-permute-start(f32[3,34,1,128]{3,2,1,0:T(1,128)S(1)} %get-tuple-element.20), channel_id=1, source_target_pairs={{0,8},{8,16},{16,24},{24,32},{32,40},{40,48},{48,56},{1,9},{9,17},... | collective-permute-start | bytes 156680 | tf_op jit(solution)/shard_map/ppermute | solution.py:24
  398.9 8.0 %collective-permute-done.18 = f32[3,34,1,128]{3,2,1,0:T(1,128)S(1)} collective-permute-done((f32[3,34,1,128]{3,2,1,0:T(1,128)S(1)}, f32[3,34,1,128]{3,2,1,0:T(1,128)S(1)}, u32[]{:S(2)}, u32[]{:S(2)}) %collective-permute-start.18) | collective-permute-done | bytes 52256 | tf_op jit(solution)/shard_map/ppermute | solution.py:25
  406.9 4.8 pad_maximum_fusion
  411.7 4.3 copy.64
  416.0 2.7 collective-permute-start.19
  418.7 1.6 collective-permute-done.19
  420.3 3.6 copy.65
  423.9 2.1 pad_maximum_fusion.24
  427.2 19.5 %all_to_all.63 = f32[8,4,64,128]{3,2,1,0:T(8,128)S(1)} all-to-all(f32[8,4,64,128]{3,2,1,0:T(8,128)S(1)} %add_add_fusion), channel_id=1, replica_groups=mesh['ta'=4,'gx'=8,'gy'=8] {'gy'}, dimensions={0} | all-to-all | bytes 2097152 | tf_op jit(solution)/shard_map/all_to_all | solution.py:72
  446.8 19.7 %fusion.48 = f32[8,4,64,128]{3,2,1,0:T(8,128)S(1)} fusion(f32[8,4,64,128]{3,2,1,0:T(8,128)S(1)} %all_to_all.63, s32[8,128]{1,0:T(8,128)S(1)} %copy-done.23, s32[8,128]{1,0:T(8,128)S(1)} %copy-done.25, f32[8,128]{1,0:T(8,128)S(1)} %copy-done.21), kind=kOutput, calls=%fused_computation.98 | convolution fusion | flops 3236954112 | bytes 2109440 | tf_op jit(solution)/shard_map/suxj,bksj->buxk/dot_general | solution.py:143
  466.4 25.3 %all_to_all.64 = f32[8,4,64,128]{3,2,1,0:T(8,128)S(1)} all-to-all(f32[8,4,64,128]{3,2,1,0:T(8,128)S(1)} %fusion.48), channel_id=1, replica_groups=mesh['ta'=4,'gx'=8,'gy'=8] {'gx'}, dimensions={0} | all-to-all | bytes 2097152 | tf_op jit(solution)/shard_map/all_to_all | solution.py:76
  491.8 9.7 %fusion.36 = f32[32,4,16,128]{3,2,1,0:T(8,128)S(1)} fusion(f32[8,4,64,128]{3,2,1,0:T(8,128)S(1)} %all_to_all.64, s32[8,64]{1,0:T(8,128)S(1)} %copy-done.27, s32[32,16]{1,0:T(8,128)S(1)} %multiply_add_fusion, f32[32,16]{1,0:T(8,128)S(1)} %copy-done.15), kind=kOutput, calls=%fused_computation.94 | convolution fusion | flops 1614544896 | bytes 2103296 | tf_op jit(solution)/shard_map/suxk,cqsx->cuqk/dot_general | solution.py:145
  501.5 44.5 %all_to_all.65 = f32[32,4,16,128]{3,2,1,0:T(8,128)S(1)} all-to-all(f32[32,4,16,128]{3,2,1,0:T(8,128)S(1)} %fusion.36), channel_id=1, replica_groups=mesh['ta'=4,'gx'=8,'gy'=8] {'ta','gy'}, dimensions={0} | all-to-all | bytes 2097152 | tf_op jit(solution)/shard_map/all_to_all | solution.py:80
  546.0 2.0 fusion.60
  547.9 1.3 fusion.207
  549.9 32.0 %all_to_all.66 = f32[32,4,16,128]{3,2,1,0:T(8,128)S(1)} all-to-all(f32[32,4,16,128]{3,2,1,0:T(8,128)S(1)} %copy.71), channel_id=1, replica_groups=mesh['ta'=4,'gx'=8,'gy'=8] {'ta','gy'}, dimensions={0} | all-to-all | bytes 2097152 | tf_op jit(solution)/shard_map/all_to_all | solution.py:80
  581.9 11.3 %fusion.42 = f32[8,4,64,128]{3,2,1,0:T(8,128)S(1)} fusion(f32[32,4,16,128]{3,2,1,0:T(8,128)S(1)} %all_to_all.66, s32[8,64]{1,0:T(8,128)S(1)} %copy-done.27, s32[32,16]{1,0:T(8,128)S(1)} %multiply_add_fusion, f32[32,16]{1,0:T(8,128)S(1)} %copy-done.15), kind=kOutput, calls=%fused_computation.96 | convolution fusion | flops 1614544896 | bytes 2103296 | tf_op jit(solution)/shard_map/cuqk,cqsx->suxk/dot_general | solution.py:153
  593.2 24.5 %all_to_all.67 = f32[8,4,64,128]{3,2,1,0:T(8,128)S(1)} all-to-all(f32[8,4,64,128]{3,2,1,0:T(8,128)S(1)} %fusion.42), channel_id=1, replica_groups=mesh['ta'=4,'gx'=8,'gy'=8] {'gx'}, dimensions={0} | all-to-all | bytes 2097152 | tf_op jit(solution)/shard_map/all_to_all | solution.py:76
  617.7 19.5 %fusion.54 = f32[8,4,64,128]{3,2,1,0:T(8,128)S(1)} fusion(s32[8,128]{1,0:T(8,128)S(1)} %copy-done.23, s32[8,128]{1,0:T(8,128)S(1)} %copy-done.25, f32[8,128]{1,0:T(8,128)S(1)} %copy-done.21, f32[8,4,64,128]{3,2,1,0:T(8,128)S(1)} %all_to_all.67), kind=kOutput, calls=%fused_computation.102 | convolution fusion | flops 3236954112 | bytes 2109440 | tf_op jit(solution)/shard_map/buxk,bksj->suxj/dot_general | solution.py:154
  637.3 25.3 %all_to_all.68 = f32[8,4,64,128]{3,2,1,0:T(8,128)S(1)} all-to-all(f32[8,4,64,128]{3,2,1,0:T(8,128)S(1)} %fusion.54), channel_id=1, replica_groups=mesh['ta'=4,'gx'=8,'gy'=8] {'gy'}, dimensions={0} | all-to-all | bytes 2097152 | tf_op jit(solution)/shard_map/all_to_all | solution.py:72
  (134 shorter events, 30.9 us)
Async XLA Ops:
  0.6 30.1 %copy-start.4 = (f32[32,64,128]{2,1,0:T(8,128)S(1)}, f32[32,64,128]{2,1,0:T(8,128)}, u32[]{:S(2)}) copy-start(f32[32,64,128]{2,1,0:T(8,128)} %param.5) | copy-start | bytes 3145732
  1.5 6.3 collective-permute-start
  2.8 6.0 collective-permute-start.1
  9.8 10.6 %collective-permute-start.2 = (f32[1,34,1,128]{3,2,1,0:T(1,128)S(1)}, f32[1,34,1,128]{3,2,1,0:T(1,128)S(1)}, u32[]{:S(2)}, u32[]{:S(2)}) collective-permute-start(f32[1,34,1,128]{3,2,1,0:T(1,128)S(1)} %get-tuple-element.50), channel_id=1, source_target_pairs={{8,0},{16,8},{24,16},{32,24},{40,32},{48,40},{56,48},{9,1},{17,9},... | collective-permute-start | bytes 52232 | tf_op jit(solution)/shard_map/ppermute | solution.py:25
  11.1 10.1 %collective-permute-start.3 = (f32[1,34,1,128]{3,2,1,0:T(1,128)S(1)}, f32[1,34,1,128]{3,2,1,0:T(1,128)S(1)}, u32[]{:S(2)}, u32[]{:S(2)}) collective-permute-start(f32[1,34,1,128]{3,2,1,0:T(1,128)S(1)} %get-tuple-element.49), channel_id=1, source_target_pairs={{0,8},{8,16},{16,24},{24,32},{32,40},{40,48},{48,56},{1,9},{9,17},... | collective-permute-start | bytes 52232 | tf_op jit(solution)/shard_map/ppermute | solution.py:24
  23.0 7.1 %collective-permute-start.4 = (f32[1,34,66,1]{2,3,1,0:T(1,128)S(1)}, f32[1,34,66,1]{2,3,1,0:T(1,128)S(1)}, u32[]{:S(2)}, u32[]{:S(2)}) collective-permute-start(f32[1,34,66,1]{2,3,1,0:T(1,128)S(1)} %copy.50), channel_id=1, source_target_pairs={{1,0},{2,1},{3,2},{4,3},{5,4},{6,5},{7,6},{9,8},{10,9},{11,10},{12... | collective-permute-start | bytes 26936 | tf_op jit(solution)/shard_map/ppermute | solution.py:25
  28.1 11.7 %copy-start.18 = (f32[32]{0:T(128)}, f32[32]{0:T(128)S(1)}, u32[]{:S(2)}) copy-start(f32[32]{0:T(128)S(1)} %compare_convert_fusion.2) | copy-start | bytes 388
  30.7 1.9 copy-start.5
  41.6 27.2 %copy-start = (f32[1,32,64,128]{3,2,1,0:T(8,128)}, f32[1,32,64,128]{3,2,1,0:T(8,128)S(1)}, u32[]{:S(2)}) copy-start(f32[1,32,64,128]{3,2,1,0:T(8,128)S(1)} %get-tuple-element.35) | copy-start | bytes 3145732
  41.6 27.2 %copy-start.1 = (f32[1,32,64,128]{3,2,1,0:T(8,128)}, f32[1,32,64,128]{3,2,1,0:T(8,128)S(1)}, u32[]{:S(2)}) copy-start(f32[1,32,64,128]{3,2,1,0:T(8,128)S(1)} %get-tuple-element.36) | copy-start | bytes 3145732
  41.6 27.2 %copy-start.2 = (f32[1,32,64,128]{3,2,1,0:T(8,128)}, f32[1,32,64,128]{3,2,1,0:T(8,128)S(1)}, u32[]{:S(2)}) copy-start(f32[1,32,64,128]{3,2,1,0:T(8,128)S(1)} %get-tuple-element.37) | copy-start | bytes 3145732
  41.6 6.3 collective-permute-start.6
  42.9 6.8 %collective-permute-start.5 = (f32[3,1,64,128]{3,2,1,0:T(8,128)S(1)}, f32[3,1,64,128]{3,2,1,0:T(8,128)S(1)}, u32[]{:S(2)}, u32[]{:S(2)}) collective-permute-start(f32[3,1,64,128]{3,2,1,0:T(8,128)S(1)} %get-tuple-element.40), channel_id=1, source_target_pairs={{0,64},{64,128},{128,192},{1,65},{65,129},{129,193},{2,66},{66,130... | collective-permute-start | bytes 294920 | tf_op jit(solution)/shard_map/ppermute | solution.py:24
  49.7 9.6 %collective-permute-start.7 = (f32[3,34,1,128]{3,2,1,0:T(1,128)S(1)}, f32[3,34,1,128]{3,2,1,0:T(1,128)S(1)}, u32[]{:S(2)}, u32[]{:S(2)}) collective-permute-start(f32[3,34,1,128]{3,2,1,0:T(1,128)S(1)} %get-tuple-element.22), channel_id=1, source_target_pairs={{0,8},{8,16},{16,24},{24,32},{32,40},{40,48},{48,56},{1,9},{9,17},... | collective-permute-start | bytes 156680 | tf_op jit(solution)/shard_map/ppermute | solution.py:24
  57.7 11.0 %collective-permute-start.8 = (f32[3,34,1,128]{3,2,1,0:T(1,128)S(1)}, f32[3,34,1,128]{3,2,1,0:T(1,128)S(1)}, u32[]{:S(2)}, u32[]{:S(2)}) collective-permute-start(f32[3,34,1,128]{3,2,1,0:T(1,128)S(1)} %get-tuple-element.23), channel_id=1, source_target_pairs={{8,0},{16,8},{24,16},{32,24},{40,32},{48,40},{56,48},{9,1},{17,9},... | collective-permute-start | bytes 156680 | tf_op jit(solution)/shard_map/ppermute | solution.py:25
  77.3 5.0 collective-permute-start.9
  85.9 3.1 copy-start.6
  85.9 3.1 copy-start.7
  85.9 3.1 copy-start.8
  85.9 3.1 copy-start.12
  85.9 3.1 copy-start.13
  91.2 21.2 %all-to-all-start = ((f32[8,4,64,128]{3,2,1,0:T(8,128)}), f32[8,4,64,128]{3,2,1,0:T(8,128)}, u32[]{:S(2)}, u32[]{:S(2)}) async-start(f32[8,4,64,128]{3,2,1,0:T(8,128)} %fusion.196), calls=%async_computation | async-start | bytes 2097152 | tf_op jit(solution)/shard_map/all_to_all | solution.py:72
  97.3 195.8 %copy-start.20 = (f32[8,128]{1,0:T(8,128)}, f32[8,128]{1,0:T(8,128)S(1)}, u32[]{:S(2)}) copy-start(f32[8,128]{1,0:T(8,128)S(1)} %multiply_sqrt_fusion.1) | copy-start | bytes 12292
  97.3 195.8 %copy-start.22 = (s32[8,128]{1,0:T(8,128)}, s32[8,128]{1,0:T(8,128)S(1)}, u32[]{:S(2)}) copy-start(s32[8,128]{1,0:T(8,128)S(1)} %get-tuple-element.58) | copy-start | bytes 12292
  97.3 195.8 %copy-start.24 = (s32[8,128]{1,0:T(8,128)}, s32[8,128]{1,0:T(8,128)S(1)}, u32[]{:S(2)}) copy-start(s32[8,128]{1,0:T(8,128)S(1)} %get-tuple-element.59) | copy-start | bytes 12292
  133.9 30.1 %all-to-all-start.1 = ((f32[8,4,64,128]{3,2,1,0:T(8,128)}), f32[8,4,64,128]{3,2,1,0:T(8,128)}, u32[]{:S(2)}, u32[]{:S(2)}) async-start(f32[8,4,64,128]{3,2,1,0:T(8,128)} %fusion.45), calls=%async_computation.1 | async-start | bytes 2097152 | tf_op jit(solution)/shard_map/all_to_all | solution.py:76
  145.6 111.8 %copy-start.26 = (s32[8,64]{1,0:T(8,128)}, s32[8,64]{1,0:T(8,128)S(1)}, u32[]{:S(2)}) copy-start(s32[8,64]{1,0:T(8,128)S(1)} %multiply_add_fusion.1) | copy-start | bytes 6148
  145.6 111.7 %copy-start.14 = (f32[32,16]{1,0:T(8,128)}, f32[32,16]{1,0:T(8,128)S(1)}, u32[]{:S(2)}) copy-start(f32[32,16]{1,0:T(8,128)S(1)} %multiply_sqrt_fusion) | copy-start | bytes 6148
  175.9 44.5 %all-to-all-start.2 = ((f32[32,4,16,128]{3,2,1,0:T(8,128)}), f32[32,4,16,128]{3,2,1,0:T(8,128)}, u32[]{:S(2)}, u32[]{:S(2)}) async-start(f32[32,4,16,128]{3,2,1,0:T(8,128)} %fusion.33), calls=%async_computation.2 | async-start | bytes 2097152 | tf_op jit(solution)/shard_map/all_to_all | solution.py:80
  193.9 31.0 %copy-start.32 = (f32[128]{0:T(128)}, f32[128]{0:T(128)S(1)}, u32[]{:S(2)}) copy-start(f32[128]{0:T(128)S(1)} %multiply_multiply_fusion.28) | copy-start | bytes 1540
  193.9 31.0 %copy-start.34 = (pred[128]{0:T(512)(128)(4,1)}, pred[128]{0:T(512)(128)(4,1)S(1)}, u32[]{:S(2)}) copy-start(pred[128]{0:T(512)(128)(4,1)S(1)} %fusion.226) | copy-start | bytes 388
  194.0 30.9 %copy-start.30 = (f32[128]{0:T(128)}, f32[128]{0:T(128)S(1)}, u32[]{:S(2)}) copy-start(f32[128]{0:T(128)S(1)} %multiply_sqrt_fusion.2) | copy-start | bytes 1540
  194.1 30.8 %copy-start.28 = (pred[128,16]{0,1:T(8,128)(4,1)}, pred[128,16]{0,1:T(8,128)(4,1)S(1)}, u32[]{:S(2)}) copy-start(pred[128,16]{0,1:T(8,128)(4,1)S(1)} %broadcast_and_fusion) | copy-start | bytes 6148
  194.2 30.8 %copy-start.16 = (f32[128,16]{0,1:T(8,128)}, f32[128,16]{0,1:T(8,128)S(1)}, u32[]{:S(2)}) copy-start(f32[128,16]{0,1:T(8,128)S(1)} %broadcast_add_fusion) | copy-start | bytes 24580
  338.2 17.8 %copy-start.3 = (f32[8,4,64,128]{3,2,1,0:T(8,128)}, f32[8,4,64,128]{3,2,1,0:T(8,128)S(1)}, u32[]{:S(2)}) copy-start(f32[8,4,64,128]{3,2,1,0:T(8,128)S(1)} %all_to_all.62) | copy-start | bytes 3145732
  338.2 28.8 %copy-start.19 = (f32[32]{0:T(128)S(1)}, f32[32]{0:T(128)}, u32[]{:S(2)}) copy-start(f32[32]{0:T(128)} %copy-done.18) | copy-start | bytes 388
  338.2 6.7 %collective-permute-start.10 = (f32[1,1,64,128]{3,2,1,0:T(8,128)S(1)}, f32[1,1,64,128]{3,2,1,0:T(8,128)S(1)}, u32[]{:S(2)}, u32[]{:S(2)}) collective-permute-start(f32[1,1,64,128]{3,2,1,0:T(8,128)S(1)} %get-tuple-element.53), channel_id=1, source_target_pairs={{64,0},{128,64},{192,128},{65,1},{129,65},{193,129},{66,2},{130,66... | collective-permute-start | bytes 98312 | tf_op jit(solution)/shard_map/ppermute | solution.py:25
  339.5 6.4 collective-permute-start.11
  345.9 9.2 %collective-permute-start.12 = (f32[1,34,1,128]{3,2,1,0:T(1,128)S(1)}, f32[1,34,1,128]{3,2,1,0:T(1,128)S(1)}, u32[]{:S(2)}, u32[]{:S(2)}) collective-permute-start(f32[1,34,1,128]{3,2,1,0:T(1,128)S(1)} %get-tuple-element.48), channel_id=1, source_target_pairs={{8,0},{16,8},{24,16},{32,24},{40,32},{48,40},{56,48},{9,1},{17,9},... | collective-permute-start | bytes 52232 | tf_op jit(solution)/shard_map/ppermute | solution.py:25
  347.2 8.8 %collective-permute-start.13 = (f32[1,34,1,128]{3,2,1,0:T(1,128)S(1)}, f32[1,34,1,128]{3,2,1,0:T(1,128)S(1)}, u32[]{:S(2)}, u32[]{:S(2)}) collective-permute-start(f32[1,34,1,128]{3,2,1,0:T(1,128)S(1)} %get-tuple-element.47), channel_id=1, source_target_pairs={{0,8},{8,16},{16,24},{24,32},{32,40},{40,48},{48,56},{1,9},{9,17},... | collective-permute-start | bytes 52232 | tf_op jit(solution)/shard_map/ppermute | solution.py:24
  358.9 6.5 collective-permute-start.14
  381.2 6.8 %collective-permute-start.16 = (f32[3,1,64,128]{3,2,1,0:T(8,128)S(1)}, f32[3,1,64,128]{3,2,1,0:T(8,128)S(1)}, u32[]{:S(2)}, u32[]{:S(2)}) collective-permute-start(f32[3,1,64,128]{3,2,1,0:T(8,128)S(1)} %get-tuple-element.33), channel_id=1, source_target_pairs={{64,0},{128,64},{192,128},{65,1},{129,65},{193,129},{66,2},{130,66... | collective-permute-start | bytes 294920 | tf_op jit(solution)/shard_map/ppermute | solution.py:25
  382.5 7.1 %collective-permute-start.15 = (f32[3,1,64,128]{3,2,1,0:T(8,128)S(1)}, f32[3,1,64,128]{3,2,1,0:T(8,128)S(1)}, u32[]{:S(2)}, u32[]{:S(2)}) collective-permute-start(f32[3,1,64,128]{3,2,1,0:T(8,128)S(1)} %get-tuple-element.32), channel_id=1, source_target_pairs={{0,64},{64,128},{128,192},{1,65},{65,129},{129,193},{2,66},{66,130... | collective-permute-start | bytes 294920 | tf_op jit(solution)/shard_map/ppermute | solution.py:24
  389.8 9.1 %collective-permute-start.17 = (f32[3,34,1,128]{3,2,1,0:T(1,128)S(1)}, f32[3,34,1,128]{3,2,1,0:T(1,128)S(1)}, u32[]{:S(2)}, u32[]{:S(2)}) collective-permute-start(f32[3,34,1,128]{3,2,1,0:T(1,128)S(1)} %get-tuple-element.20), channel_id=1, source_target_pairs={{0,8},{8,16},{16,24},{24,32},{32,40},{40,48},{48,56},{1,9},{9,17},... | collective-permute-start | bytes 156680 | tf_op jit(solution)/shard_map/ppermute | solution.py:24
  397.6 9.3 %collective-permute-start.18 = (f32[3,34,1,128]{3,2,1,0:T(1,128)S(1)}, f32[3,34,1,128]{3,2,1,0:T(1,128)S(1)}, u32[]{:S(2)}, u32[]{:S(2)}) collective-permute-start(f32[3,34,1,128]{3,2,1,0:T(1,128)S(1)} %get-tuple-element.21), channel_id=1, source_target_pairs={{8,0},{16,8},{24,16},{32,24},{40,32},{48,40},{56,48},{9,1},{17,9},... | collective-permute-start | bytes 156680 | tf_op jit(solution)/shard_map/ppermute | solution.py:25
  416.0 4.3 collective-permute-start.19
  423.9 2.2 copy-start.9
  423.9 2.2 copy-start.10
  423.9 2.2 copy-start.11
  426.1 20.6 %copy-start.21 = (f32[8,128]{1,0:T(8,128)S(1)}, f32[8,128]{1,0:T(8,128)}, u32[]{:S(2)}) copy-start(f32[8,128]{1,0:T(8,128)} %copy-done.20) | copy-start | bytes 12292
  426.1 20.6 %copy-start.23 = (s32[8,128]{1,0:T(8,128)S(1)}, s32[8,128]{1,0:T(8,128)}, u32[]{:S(2)}) copy-start(s32[8,128]{1,0:T(8,128)} %copy-done.22) | copy-start | bytes 12292
  426.1 20.6 %copy-start.25 = (s32[8,128]{1,0:T(8,128)S(1)}, s32[8,128]{1,0:T(8,128)}, u32[]{:S(2)}) copy-start(s32[8,128]{1,0:T(8,128)} %copy-done.24) | copy-start | bytes 12292
  446.7 45.0 %copy-start.15 = (f32[32,16]{1,0:T(8,128)S(1)}, f32[32,16]{1,0:T(8,128)}, u32[]{:S(2)}) copy-start(f32[32,16]{1,0:T(8,128)} %copy-done.14) | copy-start | bytes 6148
  446.7 45.0 %copy-start.27 = (s32[8,64]{1,0:T(8,128)S(1)}, s32[8,64]{1,0:T(8,128)}, u32[]{:S(2)}) copy-start(s32[8,64]{1,0:T(8,128)} %copy-done.26) | copy-start | bytes 6148
  491.7 54.2 %copy-start.17 = (f32[128,16]{0,1:T(8,128)S(1)}, f32[128,16]{0,1:T(8,128)}, u32[]{:S(2)}) copy-start(f32[128,16]{0,1:T(8,128)} %copy-done.16) | copy-start | bytes 24580
  491.7 54.2 %copy-start.29 = (pred[128,16]{0,1:T(8,128)(4,1)S(1)}, pred[128,16]{0,1:T(8,128)(4,1)}, u32[]{:S(2)}) copy-start(pred[128,16]{0,1:T(8,128)(4,1)} %copy-done.28) | copy-start | bytes 6148
  491.7 54.2 %copy-start.31 = (f32[128]{0:T(128)S(1)}, f32[128]{0:T(128)}, u32[]{:S(2)}) copy-start(f32[128]{0:T(128)} %copy-done.30) | copy-start | bytes 1540
  491.7 54.2 %copy-start.33 = (f32[128]{0:T(128)S(1)}, f32[128]{0:T(128)}, u32[]{:S(2)}) copy-start(f32[128]{0:T(128)} %copy-done.32) | copy-start | bytes 1540
  491.7 54.2 %copy-start.35 = (pred[128]{0:T(512)(128)(4,1)S(1)}, pred[128]{0:T(512)(128)(4,1)}, u32[]{:S(2)}) copy-start(pred[128]{0:T(512)(128)(4,1)} %copy-done.34) | copy-start | bytes 388
where the time goes:
time: 673 us; the launch traced here: 664 us
  blocking collectives  253 us (38%)
  matrix products  132 us (20%)
  starting transfers between devices  115 us (17%)
  waiting for transfers between devices  92.3 us (14%)
  other arithmetic  46.2 us (7%)
  local copies, waits for them, and re-layouts  23.8 us (4%)
    all_to_all x3, blocking collectives, exchange_time_y(): lax.all_to_all(blocked, ('ta', 'gy'), split_axis=0, concat_axis=0, tiled=...  108 us
    all_to_all x3, blocking collectives, exchange_x(): lax.all_to_all(blocked, 'gx', split_axis=0, concat_axis=0, tiled=True)  74.2 us
    all_to_all x3, blocking collectives, exchange_y(): lax.all_to_all(blocked, 'gy', split_axis=0, concat_axis=0, tiled=True)  70 us
    ppermute x10, starting transfers between devices, padded_2(): before = lax.ppermute(last, axis, up)  58.9 us
    dot_general x2, matrix products, on_device(): jnp.einsum('suxj,bksj->buxk', blocked, blocks_y, precision=highest)  41.1 us
    dot_general x2, matrix products, on_device(): jnp.einsum('buxk,bksj->suxj', blocked, blocks_y, precision=highest)  39.3 us
    all_to_all x1, waiting for transfers between devices, exchange_time_y(): lax.all_to_all(blocked, ('ta', 'gy'), split_axis=0, concat_axis=0, tiled=...  26.2 us
    dot_general x2, matrix products, on_device(): jnp.einsum('cuqk,cqsx->suxk', blocked, blocks_x, precision=highest)  22.7 us
  transfers between devices with their start and end apart: 23, of which 18 were waited for; matrix products, arithmetic and copies ran while one was open for 0% of the time, Pallas kernels for 0%

commit v1 on v0

v1 whole, which is shorter than its diff:
```python
import functools

import jax
import jax.numpy as jnp
import numpy as np
from jax import lax
from jax.experimental import pallas as pl
from jax.experimental.pallas import tpu as pltpu
from jax.sharding import PartitionSpec as P

NT = 128
NX = 512
NY = 1024
ITERS = 2
NEWTON = 8
ROWS = 8

MESH = pl.DeviceIdType.MESH


def cosine_table(count):
    modes = np.arange(count, dtype=np.int64)[:, None]
    cells = np.arange(count, dtype=np.int64)[None, :]
    phase = modes * (2 * cells + 1) % (4 * count)
    weight = np.where(modes == 0, 1.0, 2.0) / count
    return np.sqrt(weight) * np.cos(phase * (np.pi / (2 * count)))


def eigenvalue(count):
    return (2.0 * np.sin(np.arange(count) * (np.pi / (2 * count)))) ** 2


def matmul(left, right):
    return jnp.dot(
        left, right, precision=lax.Precision.HIGHEST, preferred_element_type=jnp.float32
    )


def middle(ref, index):
    rows, group, lanes = ref.shape
    return ref.reshape(rows * group, lanes)[pl.ds(index, rows, stride=group), :]


def set_middle(ref, index, value):
    rows, group, lanes = ref.shape
    ref.reshape(rows * group, lanes)[pl.ds(index, rows, stride=group), :] = value


def project(p0, p1, p2):
    s = p1 * p1 + p2 * p2
    half = 0.5 * s
    lam = jnp.zeros_like(p0)
    for _ in range(NEWTON):
        growth = 1.0 + lam
        cube = growth * growth * growth
        lam = jnp.maximum(lam + ((p0 - lam) * cube + half * growth) / (cube + s), 0.0)
    inverse = 1.0 / (1.0 + lam)
    return p0 - lam, p1 * inverse, p2 * inverse


def kernel(
    sizes,
    mom_in, pot_in, rho_start, rho_end, ct, ctt, cy, cyt, et, et8, ey8,
    mom_out, pot_out,
    pot, hxp, hyp, hwt, hwx, hwy, face_x, face_y, wide, wt_last, wy_all,
    src, r1, s2, r2, sp, s3, r3, s4,
    ci, cg, rip, rra, fwd_out, fwd_in, back_out, back_in,
    halo_send, halo_recv, t_send, t_recv, y_send, y_recv, p_send, p_recv,
    local_sem,
):
    A, G, B, T, X, Y = sizes
    piece = X // A
    KT = NT // B
    pieces = G * A
    chunks = piece // ROWS
    blocks = T * X // 128
    planes = 128 // X
    ta, gx, gy = (lax.axis_index(name) for name in ("ta", "gx", "gy"))
    me = gx * A + ta

    def column(k):
        other = lax.rem(me + k, pieces)
        return other, (lax.rem(other, A), other // A, gy)

    def along_t(k):
        other = lax.rem(ta + k, A)
        return other, (other, gx, gy)

    def along_y(k):
        other = lax.rem(gy + k, B)
        return other, (ta, gx, other)

    def along_x(k):
        other = lax.rem(gx + k, G)
        return other, (ta, other, gy)

    barrier = pltpu.get_barrier_semaphore()

    @pl.loop(1, pieces)
    def _(k):
        pl.semaphore_signal(barrier, inc=1, device_id=column(k)[1], device_id_type=MESH)

    @pl.loop(1, B)
    def _(k):
        pl.semaphore_signal(barrier, inc=1, device_id=along_y(k)[1], device_id_type=MESH)

    pl.semaphore_wait(barrier, pieces + B - 2)

    row_x = lax.broadcasted_iota(jnp.int32, (X, Y), 0)
    lane_x = lax.broadcasted_iota(jnp.int32, (X, Y), 1)
    eye = lax.broadcasted_iota(jnp.int32, (128, 128), 0) == lax.broadcasted_iota(
        jnp.int32, (128, 128), 1
    )

    def pack_lane(read, lane):
        def step(n, _):
            value = jnp.broadcast_to(read(n)[:, lane : lane + 1], (128, 128))
            face_y[pl.ds(n, 1), :] = jnp.sum(
                jnp.where(eye, value, 0.0), axis=0, keepdims=True
            )
            return 0

        lax.fori_loop(0, blocks, step, 0)

    def unpack_lane(read):
        def step(n, _):
            value = jnp.broadcast_to(read(n), (128, 128))
            col = jnp.sum(jnp.where(eye, value, 0.0), axis=1, keepdims=True)
            wide[pl.ds(n * planes, planes), :, :] = jnp.broadcast_to(
                col, (128, 128)
            ).reshape(planes, X, Y)
            return 0

        lax.fori_loop(0, blocks, step, 0)

    @pl.loop(0, T)
    def _(t):
        pot[0, t] = pot_in[t]

    def coefficients(j, _):
        sigma = et[pl.ds(gy * KT, KT), :] + ey8[j][0:1, :]
        lanes = pl.ds(pl.multiple_of(j * 128, 128), 128)
        g = jnp.where(me == 0, 0.0, jnp.ones_like(sigma))
        h = sigma
        for i in range(piece - 1):
            inv = 1.0 / (g + 1.0 + h)
            g = g * inv
            ci[i, :, lanes] = inv
            cg[i, :, lanes] = g
            h = sigma + h * inv
        return 0

    lax.fori_loop(0, NY // 128, coefficients, 0)

    sigma = et8[gy * (KT // 4) + me // B] + ey8[lax.rem(me, B)]
    one = jnp.ones_like(sigma)

    def inner(i, state):
        g, h, h_first, ground = state
        inv = 1.0 / (g + 1.0 + h)
        inv_first = 1.0 / (1.0 + h_first)
        return (g * inv, sigma + h * inv, sigma + h_first * inv_first, ground + g * h * inv)

    link, h_end, h_first, ground = lax.fori_loop(
        0, piece - 1, inner, (one, sigma, sigma, jnp.zeros_like(sigma))
    )

    def outer(j, s):
        inv = 1.0 / (s + link)
        rip[j] = inv
        rra[j] = link * inv
        return jnp.where(j == pieces - 2, h_end, h_end + ground) + link * s * inv

    s_last = lax.fori_loop(0, pieces - 1, outer, h_first + ground)
    rip[pieces - 1] = jnp.where(
        s_last > 0.0, 1.0 / jnp.where(s_last > 0.0, s_last, 1.0), 0.0
    )

    def sweep(it, _):
        face_x[0] = middle(pot.at[it, pl.ds(0, T)], 0)
        pack_lane(
            lambda n: pot[it, pl.ds(n * planes, planes), :, :].reshape(128, 128), 0
        )

        def faces(phase, sources, targets, step):
            copies = []
            for n, (source, target, axis) in enumerate(
                zip(sources, targets, (along_t, along_x, along_y))
            ):
                copies.append(
                    pltpu.make_async_remote_copy(
                        src_ref=source,
                        dst_ref=target,
                        send_sem=halo_send.at[it, phase, n],
                        recv_sem=halo_recv.at[it, phase, n],
                        device_id=axis(step(axis))[1],
                        device_id_type=MESH,
                    )
                )
            for copy in copies:
                copy.start()
            return copies

        size_of = {along_t: A, along_x: G, along_y: B}
        copies = faces(
            0,
            (pot.at[it, 0], face_x.at[0], face_y),
            (pot.at[it, T], hxp.at[it], hyp.at[it]),
            lambda axis: size_of[axis] - 1,
        )
        for copy in copies:
            copy.wait()
        unpack_lane(lambda n: hyp[it, pl.ds(n, 1), :])

        def plane(t, before):
            here = pot[it, t]
            last_t = (ta == A - 1) & (t == T - 1)
            slope_t = jnp.where(last_t, 0.0, pot[it, t + 1] - here)
            nxt = jnp.where(
                row_x == X - 1, hxp[it, pl.ds(t, 1), :], pltpu.roll(here, X - 1, 0)
            )
            edge_x = (row_x == X - 1) & (gx == G - 1)
            slope_x = jnp.where(edge_x, 0.0, nxt - here)
            nxt = jnp.where(lane_x == Y - 1, wide[t], pltpu.roll(here, Y - 1, 1))
            edge_y = (lane_x == Y - 1) & (gy == B - 1)
            slope_y = jnp.where(edge_y, 0.0, nxt - here)
            m0, m1, m2 = (mom_out[a, t] for a in range(3))
            q0, q1, q2 = project(slope_t + m0, slope_x + m1, slope_y + m2)
            m0, m1, m2 = (m0 + (slope_t - q0), m1 + (slope_x - q1), m2 + (slope_y - q2))
            mom_out[0, t], mom_out[1, t], mom_out[2, t] = m0, m1, m2
            wt = jnp.where(last_t, 0.0, m0 - q0)
            wx = jnp.where(edge_x, 0.0, m1 - q1)
            wy = jnp.where(edge_y, 0.0, m2 - q2)
            wy_all[t] = wy
            face_x[1, pl.ds(t, 1), :] = wx[X - 1 : X, :]
            bound = jnp.where(last_t, rho_end[...], 0.0) - jnp.where(
                (ta == 0) & (t == 0), rho_start[...], 0.0
            )
            wx_back = jnp.where(row_x == 0, 0.0, pltpu.roll(wx, 1, 0))
            wy_back = jnp.where(lane_x == 0, 0.0, pltpu.roll(wy, 1, 1))
            src[t] = wt - before + (wx - wx_back) + (wy - wy_back) + bound
            return wt

        wt_last[...] = lax.fori_loop(0, T, plane, jnp.zeros((X, Y), jnp.float32))
        pack_lane(
            lambda n: wy_all[pl.ds(n * planes, planes), :, :].reshape(128, 128), Y - 1
        )

        copies = faces(
            1,
            (wt_last, face_x.at[1], face_y),
            (hwt.at[it], hwx.at[it], hwy.at[it]),
            lambda axis: 1,
        )
        for copy in copies:
            copy.wait()
        unpack_lane(lambda n: hwy[it, pl.ds(n, 1), :])

        def fix(t, _):
            value = src[t]
            value = value - jnp.where((t == 0) & (ta > 0), hwt[it], 0.0)
            value = value - jnp.where(
                (row_x == 0) & (gx > 0), hwx[it, pl.ds(t, 1), :], 0.0
            )
            src[t] = value - jnp.where((lane_x == 0) & (gy > 0), wide[t], 0.0)
            return 0

        lax.fori_loop(0, T, fix, 0)

        def exchange(phase, axis, count, c, source, target, sends, recvs):
            own = pltpu.make_async_copy(
                source(axis(0)[0], c), target(c), local_sem.at[it, phase, c]
            )
            own.start()
            copies = []
            for k in range(1, count):
                other, where = axis(k)
                copy = pltpu.make_async_remote_copy(
                    src_ref=source(other, c),
                    dst_ref=target(c),
                    send_sem=sends.at[it, phase // 2, c, k - 1],
                    recv_sem=recvs.at[it, phase // 2, c, k - 1],
                    device_id=where,
                    device_id_type=MESH,
                )
                copy.start()
                copies.append(copy)
            return own, copies

        def landed(pair):
            own, copies = pair
            own.wait()
            for copy in copies:
                copy.wait_recv()

        def sent(pairs):
            for _, copies in pairs:
                for copy in copies:
                    copy.wait_send()

        t_out = [
            exchange(
                0, along_t, A, c,
                lambda other, c: src.at[:, pl.ds(other * piece + c * ROWS, ROWS), :],
                lambda c: r1.at[it, pl.ds(ta * T, T), pl.ds(c * ROWS, ROWS), :],
                t_send, t_recv,
            )
            for c in range(chunks)
        ]
        y_out = []
        for c in range(chunks):
            landed(t_out[c])
            for x in range(c * ROWS, (c + 1) * ROWS, 2):
                pair = jnp.concatenate(
                    [middle(r1.at[it], x + d) for d in range(2)], axis=1
                )
                pair = matmul(ct[...], pair)
                s2[x] = pair[:, :Y]
                s2[x + 1] = pair[:, Y:]
            y_out.append(
                exchange(
                    1, along_y, B, c,
                    lambda other, c: s2.at[pl.ds(c * ROWS, ROWS), pl.ds(other * KT, KT), :],
                    lambda c: r2.at[
                        it, pl.ds(c * ROWS, ROWS), :, pl.ds(pl.multiple_of(gy * Y, Y), Y)
                    ],
                    y_send, y_recv,
                )
            )
        for c in range(chunks):
            landed(y_out[c])
            lines = pl.ds(c * ROWS, ROWS)
            sp[lines] = matmul(r2[it, lines].reshape(ROWS * KT, NY), cyt[...]).reshape(
                ROWS, KT, NY
            )

        def forward(j, _):
            lanes = pl.ds(pl.multiple_of(j * 128, 128), 128)
            value = sp[0, :, lanes]
            left = jnp.zeros_like(value)
            for i in range(piece - 1):
                left = left + cg[i, :, lanes] * value
                value = sp[i + 1, :, lanes] + ci[i, :, lanes] * value
                sp[i + 1, :, lanes] = value
            for q in range(KT // 4):
                part = slice(8 * (q // 2), 8 * (q // 2) + 8)
                a, b = left[part], value[part]
                low = lax.broadcasted_iota(jnp.int32, (8, 128), 0) < 4
                if q % 2:
                    tile = jnp.where(low, pltpu.roll(a, 4, 0), b)
                else:
                    tile = jnp.where(low, a, pltpu.roll(b, 4, 0))
                fwd_out[q * B + j, 0:8, :] = tile
            return 0

        inner_sum = jnp.zeros((8, 128), jnp.float32)
        for i in range(piece - 1):
            first = 0.5 * (piece * (piece - 1) - i * (i + 1))
            other = 0.5 * (i + 1) * (piece - 1 - i)
            inner_sum = inner_sum + jnp.where(me == 0, first, other) * sp[i, 0:8, 0:128]

        @pl.loop(0, pieces)
        def _(d):
            fwd_out[d, 8:16, :] = inner_sum

        lax.fori_loop(0, NY // 128, forward, 0)

        def scatter(phase, outgoing, incoming):
            def copy_of(k):
                other, where = column(k)
                return pltpu.make_async_remote_copy(
                    src_ref=outgoing.at[other],
                    dst_ref=incoming.at[it, me],
                    send_sem=p_send.at[it, phase, k - 1],
                    recv_sem=p_recv.at[it, phase, k - 1],
                    device_id=where,
                    device_id_type=MESH,
                )

            @pl.loop(1, pieces)
            def _(k):
                copy_of(k).start()

            incoming[it, me] = outgoing[me]

            @pl.loop(1, pieces)
            def _(k):
                copy_of(k).wait()

        scatter(0, fwd_out, fwd_in)

        def down(j, state):
            value, total = state
            back_out[j, 0:8, :] = value
            total = total + fwd_in[it, j + 1, 8:16, :]
            value = (
                fwd_in[it, j + 1, 0:8, :]
                + pltpu.roll(fwd_in[it, lax.rem(j + 2, pieces), 0:8, :], 4, 0)
                * jnp.where(j + 2 < pieces, 1.0, 0.0)
                + rra[j] * value
            )
            return value, total

        start = fwd_in[it, 0, 0:8, :] + pltpu.roll(fwd_in[it, 1, 0:8, :], 4, 0)
        value, total = lax.fori_loop(
            0, pieces - 1, down, (start, fwd_in[it, 0, 8:16, :])
        )
        full = value
        value = rip[pieces - 1] * value
        low = lax.broadcasted_iota(jnp.int32, (8, 128), 0) < 4
        weighted = value * (0.5 * (piece + 1))

        def up(n, state):
            value, weighted = state
            j = pieces - 2 - n
            before = rip[j] * back_out[j, 0:8, :] + rra[j] * value
            back_out[j + 1, 0:8, :] = jnp.where(low, pltpu.roll(before, 4, 0), value)
            weighted = weighted + before * jnp.where(
                j == 0, piece + 0.5 * (piece - 1), 1.0 * piece
            )
            return before, weighted

        value, weighted = lax.fori_loop(0, pieces - 1, up, (value, weighted))
        back_out[0, 0:8, :] = jnp.where(low, 0.0, value)
        excess = pltpu.roll(full, 4, 0)
        level = -(total + pltpu.roll(weighted, 4, 0)) / NX - excess * (
            (NX * NX - 1.0) / (6.0 * NX)
        )

        @pl.loop(0, pieces)
        def _(d):
            back_out[d, 8:16, :] = excess
            back_out[d, 16:24, :] = level

        scatter(1, back_out, back_in)

        def backward(j, _):
            lanes = pl.ds(pl.multiple_of(j * 128, 128), 128)
            left, value = [], []
            for half in range(KT // 8):
                a = back_in[it, 2 * half * B + j, 0:8, :]
                b = back_in[it, (2 * half + 1) * B + j, 0:8, :]
                left.append(jnp.where(low, a, pltpu.roll(b, 4, 0)))
                value.append(jnp.where(low, pltpu.roll(a, 4, 0), b))
            left = jnp.concatenate(left, axis=0)
            value = jnp.concatenate(value, axis=0)
            sp[piece - 1, :, lanes] = value
            for i in range(piece - 2, -1, -1):
                value = ci[i, :, lanes] * (sp[i, :, lanes] + value) + cg[i, :, lanes] * left
                sp[i, :, lanes] = value
            return 0

        lax.fori_loop(0, NY // 128, backward, 0)
        constant = (
            (gy == 0)
            & (lax.broadcasted_iota(jnp.int32, (8, 128), 0) == 0)
            & (lax.broadcasted_iota(jnp.int32, (8, 128), 1) == 0)
        )
        excess = back_in[it, 0, 8:16, :]
        level = back_in[it, 0, 16:24, :]
        for i in range(piece):
            cell = (me * piece + i).astype(jnp.float32)
            ramp = cell * (cell + 1.0) * (0.5 / NX)
            sp[i, 0:8, 0:128] += jnp.where(constant, excess * ramp + level, 0.0)

        y_back = []
        for c in range(chunks):
            lines = pl.ds(c * ROWS, ROWS)
            s3[lines] = matmul(sp[lines].reshape(ROWS * KT, NY), cy[...]).reshape(
                ROWS, KT, NY
            )
            y_back.append(
                exchange(
                    3, along_y, B, c,
                    lambda other, c: s3.at[
                        pl.ds(c * ROWS, ROWS), :, pl.ds(pl.multiple_of(other * Y, Y), Y)
                    ],
                    lambda c: r3.at[it, pl.ds(c * ROWS, ROWS), pl.ds(gy * KT, KT), :],
                    y_send, y_recv,
                )
            )
        t_back = []
        for c in range(chunks):
            landed(y_back[c])
            for x in range(c * ROWS, (c + 1) * ROWS, 2):
                pair = jnp.concatenate([r3[it, x + d] for d in range(2)], axis=1)
                pair = matmul(ctt[...], pair)
                set_middle(s4, x, pair[:, :Y])
                set_middle(s4, x + 1, pair[:, Y:])
            t_back.append(
                exchange(
                    2, along_t, A, c,
                    lambda other, c: s4.at[pl.ds(other * T, T), pl.ds(c * ROWS, ROWS), :],
                    lambda c: pot.at[
                        it + 1, pl.ds(0, T), pl.ds(ta * piece + c * ROWS, ROWS), :
                    ],
                    t_send, t_recv,
                )
            )
        for pair in t_back:
            landed(pair)
        for pairs in (t_out, y_out, y_back, t_back):
            sent(pairs)
        return 0

    @pl.loop(0, T)
    def _(t):
        for a in range(3):
            mom_out[a, t] = mom_in[a, t]

    lax.fori_loop(0, ITERS, sweep, 0)

    @pl.loop(0, T)
    def _(t):
        pot_out[t] = pot[ITERS, t]


def on_device(sizes, momenta, potential, rho_start, rho_end):
    A, G, B, T, X, Y = sizes
    piece, KT, pieces = X // A, NT // B, G * A
    assert Y == 128 and 128 % X == 0 and T * X % 128 == 0 and piece % ROWS == 0
    assert KT % 8 == 0 and pieces == (KT // 4) * B
    chunks = piece // ROWS
    table_t = cosine_table(NT).astype(np.float32)
    table_y = cosine_table(NY).astype(np.float32)
    e_t = eigenvalue(NT)
    spread_t = np.broadcast_to(e_t[:, None], (NT, 128)).astype(np.float32)
    spread_8 = np.broadcast_to(
        np.concatenate([e_t.reshape(NT // 4, 4)] * 2, axis=1)[:, :, None], (NT // 4, 8, 128)
    ).astype(np.float32)
    spread_y = np.broadcast_to(
        eigenvalue(NY).reshape(B, 1, 128), (B, 8, 128)
    ).astype(np.float32)
    tables = [table_t, table_t.T, table_y, table_y.T, spread_t, spread_8, spread_y]
    operands = [momenta, potential, rho_start, rho_end] + [
        jnp.asarray(np.ascontiguousarray(table)) for table in tables
    ]
    f32 = jnp.float32
    face = max(T * X // 128, 8)
    vmem = pl.BlockSpec(memory_space=pltpu.VMEM)
    dma = pltpu.SemaphoreType.DMA
    return pl.pallas_call(
        functools.partial(kernel, sizes),
        out_shape=(
            jax.ShapeDtypeStruct(momenta.shape, f32),
            jax.ShapeDtypeStruct(potential.shape, f32),
        ),
        in_specs=[vmem] * len(operands),
        out_specs=(vmem, vmem),
        scratch_shapes=[
            pltpu.VMEM((ITERS + 1, T + 1, X, Y), f32),
            pltpu.VMEM((ITERS, T, Y), f32),
            pltpu.VMEM((ITERS, face, 128), f32),
            pltpu.VMEM((ITERS, X, Y), f32),
            pltpu.VMEM((ITERS, T, Y), f32),
            pltpu.VMEM((ITERS, face, 128), f32),
            pltpu.VMEM((2, T, Y), f32),
            pltpu.VMEM((face, 128), f32),
            pltpu.VMEM((T, X, Y), f32),
            pltpu.VMEM((X, Y), f32),
            pltpu.VMEM((T, X, Y), f32),
            pltpu.VMEM((T, X, Y), f32),
            pltpu.VMEM((ITERS, NT, piece, Y), f32),
            pltpu.VMEM((piece, NT, Y), f32),
            pltpu.VMEM((ITERS, piece, KT, NY), f32),
            pltpu.VMEM((piece, KT, NY), f32),
            pltpu.VMEM((piece, KT, NY), f32),
            pltpu.VMEM((ITERS, piece, NT, Y), f32),
            pltpu.VMEM((NT, piece, Y), f32),
            pltpu.VMEM((piece, KT, NY), f32),
            pltpu.VMEM((piece, KT, NY), f32),
            pltpu.VMEM((pieces, 8, 128), f32),
            pltpu.VMEM((pieces, 8, 128), f32),
            pltpu.VMEM((pieces, 16, 128), f32),
            pltpu.VMEM((ITERS, pieces, 16, 128), f32),
            pltpu.VMEM((pieces, 24, 128), f32),
            pltpu.VMEM((ITERS, pieces, 24, 128), f32),
            dma((ITERS, 2, 3)),
            dma((ITERS, 2, 3)),
            dma((ITERS, 2, chunks, A - 1)),
            dma((ITERS, 2, chunks, A - 1)),
            dma((ITERS, 2, chunks, B - 1)),
            dma((ITERS, 2, chunks, B - 1)),
            dma((ITERS, 2, pieces - 1)),
            dma((ITERS, 2, pieces - 1)),
            dma((ITERS, 4, chunks)),
        ],
        compiler_params=pltpu.CompilerParams(
            collective_id=0, has_side_effects=True, vmem_limit_bytes=56 << 20
        ),
    )(*operands)


def solution(mesh):
    A, G, B = (mesh.shape[name] for name in ("ta", "gx", "gy"))
    sizes = (A, G, B, NT // A, NX // G, NY // B)
    placed = (P(None, "ta", "gx", "gy"), P("ta", "gx", "gy"), P("gx", "gy"), P("gx", "gy"))
    return jax.shard_map(
        functools.partial(on_device, sizes),
        mesh=mesh,
        in_specs=placed,
        out_specs=(P(None, "ta", "gx", "gy"), P("ta", "gx", "gy")),
        check_vma=False,
    )
```

time: 673 us -> 263 us (0.39); the launches traced: 664 us -> 263 us
  Pallas kernels: 0 us -> 257 us
  blocking collectives: 253 us -> 0 us
  matrix products: 132 us -> 0 us
  starting transfers between devices: 115 us -> 0 us
  waiting for transfers between devices: 92.3 us -> 0 us
  other arithmetic: 46.2 us -> 0 us
  local copies, waits for them, and re-layouts: 23.8 us -> 5.03 us
    pallas_call x0 -> x1, Pallas kernels: none -> 257 us  [on_device(): pl.pallas_call(functools.partial(kernel, sizes), out_shape=(jax.ShapeDtyp...]
    all_to_all x9 -> x0, blocking collectives: 253 us -> none  [the longest x3 108 us: exchange_time_y(): lax.all_to_all(blocked, ('ta', 'gy'), split_axis=0, concat_axis=0, tiled=...]
    dot_general x12 -> x0, matrix products: 132 us -> none  [the longest x2 41.1 us: on_device(): jnp.einsum('suxj,bksj->buxk', blocked, blocks_y, precision=highest)]
    ppermute x20 -> x0, starting transfers between devices: 79.2 us -> none  [the longest x10 58.9 us: padded_2(): before = lax.ppermute(last, axis, up)]
    all_to_all x3 -> x0, waiting for transfers between devices: 59.7 us -> none  [the longest x1 26.2 us: exchange_time_y(): lax.all_to_all(blocked, ('ta', 'gy'), split_axis=0, concat_axis=0, tiled=...]
    all_to_all x3 -> x0, starting transfers between devices: 35.6 us -> none  [the longest x1 17.8 us: exchange_time_y(): lax.all_to_all(blocked, ('ta', 'gy'), split_axis=0, concat_axis=0, tiled=...]
    ppermute x20 -> x0, waiting for transfers between devices: 32.6 us -> none  [the longest x10 22.4 us: padded_2(): after = lax.ppermute(first, axis, down)]
    concatenate x8 -> x0, other arithmetic: 18.3 us -> none  [padded_2(): array = jnp.concatenate([before, array, after], axis=dim)]
  transfers between devices with their start and end apart: 23 -> 0, of which waited for: 18 -> 0; matrix products, arithmetic and copies ran while one was open for 0% -> 0% of each run, Pallas kernels for 0% -> 0%
where the time goes in v1:
time: 263 us
  Pallas kernels  257 us (98%)
  local copies, waits for them, and re-layouts  5.03 us (2%)
    pallas_call x1, Pallas kernels, on_device(): pl.pallas_call(functools.partial(kernel, sizes), out_shape=(jax.ShapeDtyp...  257 us

profile of v1, /device:TPU:1, one launch (start us, length us, event | category | flops | bytes accessed | tf_op | source)
XLA Modules:
  0.0 263.0 jit_solution(5111521870536062134)
XLA Ops:
  0.6 257.3 %shard_map.122 = (f32[3,32,64,128]{3,2,1,0:T(8,128)}, f32[32,64,128]{2,1,0:T(8,128)}) custom-call(f32[3,32,64,128]{3,2,1,0:T(8,128)} %mom_in.1, f32[32,64,128]{2,1,0:T(8,128)} %pot_in.1, f32[64,128]{1,0:T(8,128)} %rho_start.1, f32[64,128]{1,0:T(8,128)} %rho_end.1, f32[128,128]{1,0:T(8,128)} %constant.14.clone.ct, f32[128,128]{1,0:T(8,128)} %constant.15.clone.ctt, ...), custom_call_target="tpu_custom_call" | custom-call | tf_op jit(solution)/shard_map/pallas_call | solution.py:542
  257.9 0.0 copy-start
  257.9 4.1 %copy.15 = f32[3,32,64,128]{3,2,1,0:T(8,128)} copy(f32[3,32,64,128]{3,2,1,0:T(8,128)} %get-tuple-element.4) | data formatting | bytes 6291456
  262.0 0.0 copy-done
  262.0 1.0 copy.16
Async XLA Ops:
  257.9 4.1 %copy-start = (f32[32,64,128]{2,1,0:T(8,128)S(1)}, f32[32,64,128]{2,1,0:T(8,128)}, u32[]{:S(2)}) copy-start(f32[32,64,128]{2,1,0:T(8,128)} %get-tuple-element.5) | copy-start | bytes 3145732

commit v2 on v1

--- a/solution.py
+++ b/solution.py
@@ -64,8 +64,8 @@
     mom_out, pot_out,
     pot, hxp, hyp, hwt, hwx, hwy, face_x, face_y, wide, wt_last, wy_all,
     src, r1, s2, r2, sp, s3, r3, s4,
-    ci, cg, rip, rra, fwd_out, fwd_in, back_out, back_in,
-    halo_send, halo_recv, t_send, t_recv, y_send, y_recv, p_send, p_recv,
+    ci, cg, rip, rra, fwd_out, fwd_in, back_out, back_in, extra_out, extra_in,
+    halo_send, halo_recv, t_send, t_recv, y_send, y_recv, p_send, p_recv, e_send, e_recv,
     local_sem,
 ):
     A, G, B, T, X, Y = sizes
@@ -75,6 +75,7 @@
     chunks = piece // ROWS
     blocks = T * X // 128
     planes = 128 // X
+    unroll = min(blocks, 4)
     ta, gx, gy = (lax.axis_index(name) for name in ("ta", "gx", "gy"))
     me = gx * A + ta
 
@@ -113,68 +114,73 @@
     )
 
     def pack_lane(read, lane):
-        def step(n, _):
-            value = jnp.broadcast_to(read(n)[:, lane : lane + 1], (128, 128))
-            face_y[pl.ds(n, 1), :] = jnp.sum(
-                jnp.where(eye, value, 0.0), axis=0, keepdims=True
-            )
+        def step(group, _):
+            for u in range(unroll):
+                n = group * unroll + u
+                value = jnp.broadcast_to(read(n)[:, lane : lane + 1], (128, 128))
+                face_y[pl.ds(n, 1), :] = jnp.sum(
+                    jnp.where(eye, value, 0.0), axis=0, keepdims=True
+                )
             return 0
 
-        lax.fori_loop(0, blocks, step, 0)
+        lax.fori_loop(0, blocks // unroll, step, 0)
 
     def unpack_lane(read):
-        def step(n, _):
-            value = jnp.broadcast_to(read(n), (128, 128))
-            col = jnp.sum(jnp.where(eye, value, 0.0), axis=1, keepdims=True)
-            wide[pl.ds(n * planes, planes), :, :] = jnp.broadcast_to(
-                col, (128, 128)
-            ).reshape(planes, X, Y)
+        def step(group, _):
+            for u in range(unroll):
+                n = group * unroll + u
+                value = jnp.broadcast_to(read(n), (128, 128))
+                col = jnp.sum(jnp.where(eye, value, 0.0), axis=1, keepdims=True)
+                wide[pl.ds(n * planes, planes), :, :] = jnp.broadcast_to(
+                    col, (128, 128)
+                ).reshape(planes, X, Y)
             return 0
 
-        lax.fori_loop(0, blocks, step, 0)
+        lax.fori_loop(0, blocks // unroll, step, 0)
 
     @pl.loop(0, T)
     def _(t):
         pot[0, t] = pot_in[t]
 
-    def coefficients(j, _):
-        sigma = et[pl.ds(gy * KT, KT), :] + ey8[j][0:1, :]
-        lanes = pl.ds(pl.multiple_of(j * 128, 128), 128)
-        g = jnp.where(me == 0, 0.0, jnp.ones_like(sigma))
-        h = sigma
-        for i in range(piece - 1):
+    def prepare():
+        def coefficients(j, _):
+            sigma = et[pl.ds(gy * KT, KT), :] + ey8[j][0:1, :]
+            lanes = pl.ds(pl.multiple_of(j * 128, 128), 128)
+            g = jnp.where(me == 0, 0.0, jnp.ones_like(sigma))
+            h = sigma
+            for i in range(piece - 1):
+                inv = 1.0 / (g + 1.0 + h)
+                g = g * inv
+                ci[i, :, lanes] = inv
+                cg[i, :, lanes] = g
+                h = sigma + h * inv
+            return 0
+
+        lax.fori_loop(0, NY // 128, coefficients, 0)
+
+        sigma = et8[gy * (KT // 4) + me // B] + ey8[lax.rem(me, B)]
+        one = jnp.ones_like(sigma)
+
+        def inner(i, state):
+            g, h, h_first, ground = state
             inv = 1.0 / (g + 1.0 + h)
-            g = g * inv
-            ci[i, :, lanes] = inv
-            cg[i, :, lanes] = g
-            h = sigma + h * inv
-        return 0
-
-    lax.fori_loop(0, NY // 128, coefficients, 0)
-
-    sigma = et8[gy * (KT // 4) + me // B] + ey8[lax.rem(me, B)]
-    one = jnp.ones_like(sigma)
-
-    def inner(i, state):
-        g, h, h_first, ground = state
-        inv = 1.0 / (g + 1.0 + h)
-        inv_first = 1.0 / (1.0 + h_first)
-        return (g * inv, sigma + h * inv, sigma + h_first * inv_first, ground + g * h * inv)
-
-    link, h_end, h_first, ground = lax.fori_loop(
-        0, piece - 1, inner, (one, sigma, sigma, jnp.zeros_like(sigma))
-    )
-
-    def outer(j, s):
-        inv = 1.0 / (s + link)
-        rip[j] = inv
-        rra[j] = link * inv
-        return jnp.where(j == pieces - 2, h_end, h_end + ground) + link * s * inv
-
-    s_last = lax.fori_loop(0, pieces - 1, outer, h_first + ground)
-    rip[pieces - 1] = jnp.where(
-        s_last > 0.0, 1.0 / jnp.where(s_last > 0.0, s_last, 1.0), 0.0
-    )
+            inv_first = 1.0 / (1.0 + h_first)
+            return (g * inv, sigma + h * inv, sigma + h_first * inv_first, ground + g * h * inv)
+
+        link, h_end, h_first, ground = lax.fori_loop(
+            0, piece - 1, inner, (one, sigma, sigma, jnp.zeros_like(sigma))
+        )
+
+        def outer(j, s):
+            inv = 1.0 / (s + link)
+            rip[j] = inv
+            rra[j] = link * inv
+            return jnp.where(j == pieces - 2, h_end, h_end + ground) + link * s * inv
+
+        s_last = lax.fori_loop(0, pieces - 1, outer, h_first + ground)
+        rip[pieces - 1] = jnp.where(
+            s_last > 0.0, 1.0 / jnp.where(s_last > 0.0, s_last, 1.0), 0.0
+        )
 
     def sweep(it, _):
         face_x[0] = middle(pot.at[it, pl.ds(0, T)], 0)
@@ -208,6 +214,7 @@
             (pot.at[it, T], hxp.at[it], hyp.at[it]),
             lambda axis: size_of[axis] - 1,
         )
+        pl.when(it == 0)(prepare)
         for copy in copies:
             copy.wait()
         unpack_lane(lambda n: hyp[it, pl.ds(n, 1), :])
@@ -350,7 +357,7 @@
                     tile = jnp.where(low, pltpu.roll(a, 4, 0), b)
                 else:
                     tile = jnp.where(low, a, pltpu.roll(b, 4, 0))
-                fwd_out[q * B + j, 0:8, :] = tile
+                fwd_out[q * B + j] = tile
             return 0
 
         inner_sum = jnp.zeros((8, 128), jnp.float32)
@@ -359,87 +366,122 @@
             other = 0.5 * (i + 1) * (piece - 1 - i)
             inner_sum = inner_sum + jnp.where(me == 0, first, other) * sp[i, 0:8, 0:128]
 
-        @pl.loop(0, pieces)
-        def _(d):
-            fwd_out[d, 8:16, :] = inner_sum
-
+        extra_out[0] = inner_sum
         lax.fori_loop(0, NY // 128, forward, 0)
 
+        partners = [(dx, dt) for dx in range(G) for dt in range(A)][1:]
+        to_x = [lax.rem(gx + d, G) for d in range(G)]
+        to_t = [lax.rem(ta + d, A) for d in range(A)]
+
         def scatter(phase, outgoing, incoming):
-            def copy_of(k):
-                other, where = column(k)
-                return pltpu.make_async_remote_copy(
-                    src_ref=outgoing.at[other],
-                    dst_ref=incoming.at[it, me],
-                    send_sem=p_send.at[it, phase, k - 1],
-                    recv_sem=p_recv.at[it, phase, k - 1],
-                    device_id=where,
-                    device_id_type=MESH,
-                )
+            copies = []
+            for n, (dx, dt) in enumerate(partners):
+                copies.append(
+                    pltpu.make_async_remote_copy(
+                        src_ref=outgoing.at[to_x[dx] * A + to_t[dt]],
+                        dst_ref=incoming.at[it, me],
+                        send_sem=p_send.at[it, phase, n],
+                        recv_sem=p_recv.at[it, phase, n],
+                        device_id=(to_t[dt], to_x[dx], gy),
+                        device_id_type=MESH,
+                    )
+                )
+            for copy in copies:
+                copy.start()
+            incoming[it, me] = outgoing[me]
+            return copies
+
+        def gather_copy(k):
+            return pltpu.make_async_remote_copy(
+                src_ref=extra_out.at[0],
+                dst_ref=extra_in.at[it, k],
+                send_sem=e_send.at[it, k],
+                recv_sem=e_recv.at[it, k],
+                device_id=(0, 0, gy),
+                device_id_type=MESH,
+            )
+
+        def spread_copy(k):
+            return pltpu.make_async_remote_copy(
+                src_ref=extra_out.at[1],
+                dst_ref=extra_in.at[it, pieces],
+                send_sem=e_send.at[it, k],
+                recv_sem=e_recv.at[it, pieces],
+                device_id=(lax.rem(k, A), k // A, gy),
+                device_id_type=MESH,
+            )
+
+        head = (gy == 0) & (me == 0)
+        tail = (gy == 0) & (me > 0)
+        copies = scatter(0, fwd_out, fwd_in)
+
+        @pl.when(tail)
+        def _():
+            gather_copy(me).start()
+
+        @pl.when(head)
+        def _():
+            extra_in[it, 0] = extra_out[0]
 
             @pl.loop(1, pieces)
             def _(k):
-                copy_of(k).start()
-
-            incoming[it, me] = outgoing[me]
+                gather_copy(k).wait_recv()
+
+        for copy in copies:
+            copy.wait_recv()
+
+        low = lax.broadcasted_iota(jnp.int32, (8, 128), 0) < 4
+        value = fwd_in[it, 0] + pltpu.roll(fwd_in[it, 1], 4, 0)
+        before = [value]
+        for j in range(1, pieces):
+            given = fwd_in[it, j]
+            if j + 1 < pieces:
+                given = given + pltpu.roll(fwd_in[it, j + 1], 4, 0)
+            value = given + rra[j - 1] * value
+            before.append(value)
+        full = value
+        value = rip[pieces - 1] * value
+        weighted = value * (0.5 * (piece + 1))
+        for j in range(pieces - 2, -1, -1):
+            here = rip[j] * before[j] + rra[j] * value
+            back_out[j + 1] = jnp.where(low, pltpu.roll(here, 4, 0), value)
+            value = here
+            weighted = weighted + value * (
+                piece + 0.5 * (piece - 1) if j == 0 else 1.0 * piece
+            )
+        back_out[0] = jnp.where(low, 0.0, value)
+        returns = scatter(1, back_out, back_in)
+
+        @pl.when(head)
+        def _():
+            total = lax.fori_loop(
+                1, pieces, lambda k, acc: acc + extra_in[it, k], extra_in[it, 0]
+            )
+            excess = pltpu.roll(full, 4, 0)
+            level = -(total + pltpu.roll(weighted, 4, 0)) / NX - excess * (
+                (NX * NX - 1.0) / (6.0 * NX)
+            )
+            row = lax.broadcasted_iota(jnp.int32, (8, 128), 0)
+            extra_out[1] = jnp.where(row == 0, excess, pltpu.roll(level, 1, 0))
+            extra_in[it, pieces] = extra_out[1]
 
             @pl.loop(1, pieces)
             def _(k):
-                copy_of(k).wait()
-
-        scatter(0, fwd_out, fwd_in)
-
-        def down(j, state):
-            value, total = state
-            back_out[j, 0:8, :] = value
-            total = total + fwd_in[it, j + 1, 8:16, :]
-            value = (
-                fwd_in[it, j + 1, 0:8, :]
-                + pltpu.roll(fwd_in[it, lax.rem(j + 2, pieces), 0:8, :], 4, 0)
-                * jnp.where(j + 2 < pieces, 1.0, 0.0)
-                + rra[j] * value
-            )
-            return value, total
-
-        start = fwd_in[it, 0, 0:8, :] + pltpu.roll(fwd_in[it, 1, 0:8, :], 4, 0)
-        value, total = lax.fori_loop(
-            0, pieces - 1, down, (start, fwd_in[it, 0, 8:16, :])
-        )
-        full = value
-        value = rip[pieces - 1] * value
-        low = lax.broadcasted_iota(jnp.int32, (8, 128), 0) < 4
-        weighted = value * (0.5 * (piece + 1))
-
-        def up(n, state):
-            value, weighted = state
-            j = pieces - 2 - n
-            before = rip[j] * back_out[j, 0:8, :] + rra[j] * value
-            back_out[j + 1, 0:8, :] = jnp.where(low, pltpu.roll(before, 4, 0), value)
-            weighted = weighted + before * jnp.where(
-                j == 0, piece + 0.5 * (piece - 1), 1.0 * piece
-            )
-            return before, weighted
-
-        value, weighted = lax.fori_loop(0, pieces - 1, up, (value, weighted))
-        back_out[0, 0:8, :] = jnp.where(low, 0.0, value)
-        excess = pltpu.roll(full, 4, 0)
-        level = -(total + pltpu.roll(weighted, 4, 0)) / NX - excess * (
-            (NX * NX - 1.0) / (6.0 * NX)
-        )
-
-        @pl.loop(0, pieces)
-        def _(d):
-            back_out[d, 8:16, :] = excess
-            back_out[d, 16:24, :] = level
-
-        scatter(1, back_out, back_in)
+                spread_copy(k).start()
+
+        for copy in returns:
+            copy.wait_recv()
+
+        @pl.when(tail)
+        def _():
+            spread_copy(me).wait_recv()
 
         def backward(j, _):
             lanes = pl.ds(pl.multiple_of(j * 128, 128), 128)
             left, value = [], []
             for half in range(KT // 8):
-                a = back_in[it, 2 * half * B + j, 0:8, :]
-                b = back_in[it, (2 * half + 1) * B + j, 0:8, :]
+                a = back_in[it, 2 * half * B + j]
+                b = back_in[it, (2 * half + 1) * B + j]
                 left.append(jnp.where(low, a, pltpu.roll(b, 4, 0)))
                 value.append(jnp.where(low, pltpu.roll(a, 4, 0), b))
             left = jnp.concatenate(left, axis=0)
@@ -451,17 +493,17 @@
             return 0
 
         lax.fori_loop(0, NY // 128, backward, 0)
-        constant = (
-            (gy == 0)
-            & (lax.broadcasted_iota(jnp.int32, (8, 128), 0) == 0)
-            & (lax.broadcasted_iota(jnp.int32, (8, 128), 1) == 0)
-        )
-        excess = back_in[it, 0, 8:16, :]
-        level = back_in[it, 0, 16:24, :]
-        for i in range(piece):
-            cell = (me * piece + i).astype(jnp.float32)
-            ramp = cell * (cell + 1.0) * (0.5 / NX)
-            sp[i, 0:8, 0:128] += jnp.where(constant, excess * ramp + level, 0.0)
+
+        @pl.when(gy == 0)
+        def _():
+            row = lax.broadcasted_iota(jnp.int32, (8, 128), 0)
+            constant = (row == 0) & (lax.broadcasted_iota(jnp.int32, (8, 128), 1) == 0)
+            excess = extra_in[it, pieces]
+            level = pltpu.roll(excess, 7, 0)
+            for i in range(piece):
+                cell = (me * piece + i).astype(jnp.float32)
+                ramp = cell * (cell + 1.0) * (0.5 / NX)
+                sp[i, 0:8, 0:128] += jnp.where(constant, excess * ramp + level, 0.0)
 
         y_back = []
         for c in range(chunks):
@@ -501,6 +543,19 @@
             landed(pair)
         for pairs in (t_out, y_out, y_back, t_back):
             sent(pairs)
+        for copy in copies + returns:
+            copy.wait_send()
+
+        @pl.when(tail)
+        def _():
+            gather_copy(me).wait_send()
+
+        @pl.when(head)
+        def _():
+            @pl.loop(1, pieces)
+            def _(k):
+                spread_copy(k).wait_send()
+
         return 0
 
     @pl.loop(0, T)
@@ -571,10 +626,12 @@
             pltpu.VMEM((piece, KT, NY), f32),
             pltpu.VMEM((pieces, 8, 128), f32),
             pltpu.VMEM((pieces, 8, 128), f32),
-            pltpu.VMEM((pieces, 16, 128), f32),
-            pltpu.VMEM((ITERS, pieces, 16, 128), f32),
-            pltpu.VMEM((pieces, 24, 128), f32),
-            pltpu.VMEM((ITERS, pieces, 24, 128), f32),
+            pltpu.VMEM((pieces, 8, 128), f32),
+            pltpu.VMEM((ITERS, pieces, 8, 128), f32),
+            pltpu.VMEM((pieces, 8, 128), f32),
+            pltpu.VMEM((ITERS, pieces, 8, 128), f32),
+            pltpu.VMEM((2, 8, 128), f32),
+            pltpu.VMEM((ITERS, pieces + 1, 8, 128), f32),
             dma((ITERS, 2, 3)),
             dma((ITERS, 2, 3)),
             dma((ITERS, 2, chunks, A - 1)),
@@ -583,6 +640,8 @@
             dma((ITERS, 2, chunks, B - 1)),
             dma((ITERS, 2, pieces - 1)),
             dma((ITERS, 2, pieces - 1)),
+            dma((ITERS, pieces)),
+            dma((ITERS, pieces + 1)),
             dma((ITERS, 4, chunks)),
         ],
         compiler_params=pltpu.CompilerParams(

time: 263 us -> 243 us (0.924)
  Pallas kernels: 257 us -> 237 us
    pallas_call x1, Pallas kernels: 257 us -> 237 us  [on_device(): pl.pallas_call(functools.partial(kernel, sizes), out_shape=(jax.ShapeDtyp...]
where the time goes in v2:
time: 243 us
  Pallas kernels  237 us (98%)
  local copies, waits for them, and re-layouts  5.03 us (2%)
    pallas_call x1, Pallas kernels, on_device(): pl.pallas_call(functools.partial(kernel, sizes), out_shape=(jax.ShapeDtyp...  237 us
    unnamed x4, local copies, waits for them, and re-layouts  5.03 us

profile of v2, /device:TPU:1, one launch (start us, length us, event | category | flops | bytes accessed | tf_op | source)
XLA Modules:
  0.0 242.6 jit_solution(14440693927790023313)
XLA Ops:
  0.6 236.9 %shard_map.122 = (f32[3,32,64,128]{3,2,1,0:T(8,128)}, f32[32,64,128]{2,1,0:T(8,128)}) custom-call(f32[3,32,64,128]{3,2,1,0:T(8,128)} %mom_in.1, f32[32,64,128]{2,1,0:T(8,128)} %pot_in.1, f32[64,128]{1,0:T(8,128)} %rho_start.1, f32[64,128]{1,0:T(8,128)} %rho_end.1, f32[128,128]{1,0:T(8,128)} %constant.14.clone.ct, f32[128,128]{1,0:T(8,128)} %constant.15.clone.ctt, ...), custom_call_target="tpu_custom_call" | custom-call | tf_op jit(solution)/shard_map/pallas_call | solution.py:597
  237.5 0.0 copy-start
  237.5 4.1 %copy.15 = f32[3,32,64,128]{3,2,1,0:T(8,128)} copy(f32[3,32,64,128]{3,2,1,0:T(8,128)} %get-tuple-element.4) | data formatting | bytes 6291456
  241.6 0.0 copy-done
  241.6 1.0 copy.16
Async XLA Ops:
  237.5 4.1 %copy-start = (f32[32,64,128]{2,1,0:T(8,128)S(1)}, f32[32,64,128]{2,1,0:T(8,128)}, u32[]{:S(2)}) copy-start(f32[32,64,128]{2,1,0:T(8,128)} %get-tuple-element.5) | copy-start | bytes 3145732

commit v3 on v2

v3 whole, which is shorter than its diff:
```python
import functools

import jax
import jax.numpy as jnp
import numpy as np
from jax import lax
from jax.experimental import pallas as pl
from jax.experimental.pallas import tpu as pltpu
from jax.sharding import PartitionSpec as P

NT = 128
NX = 512
NY = 1024
ITERS = 2
NEWTON = 8
ROWS = 4

MESH = pl.DeviceIdType.MESH


def cosine_table(count):
    modes = np.arange(count, dtype=np.int64)[:, None]
    cells = np.arange(count, dtype=np.int64)[None, :]
    phase = modes * (2 * cells + 1) % (4 * count)
    weight = np.where(modes == 0, 1.0, 2.0) / count
    return np.sqrt(weight) * np.cos(phase * (np.pi / (2 * count)))


def eigenvalue(count):
    return (2.0 * np.sin(np.arange(count) * (np.pi / (2 * count)))) ** 2


def split(value):
    parts = []
    for _ in range(3):
        part = value.astype(jnp.bfloat16)
        parts.append(part)
        value = value - part.astype(jnp.float32)
    return parts


def product(left, right):
    return jnp.dot(left, right, preferred_element_type=jnp.float32)


def table_right(value, table):
    rows = value.shape[0]
    parts = split(value)
    total = product(parts[0], table[2])
    middle_ = product(jnp.concatenate(parts[:2], axis=0), table[1])
    large = product(jnp.concatenate(parts, axis=0), table[0])
    total = total + (middle_[rows:] + large[2 * rows :])
    total = total + (middle_[:rows] + large[rows : 2 * rows])
    return total + large[:rows]


def table_left(table, value):
    rows = table.shape[0] // 3
    parts = split(value)
    total = product(table[:rows], parts[2])
    middle_ = product(table[: 2 * rows], parts[1])
    large = product(table[...], parts[0])
    total = total + (middle_[rows:] + large[2 * rows :])
    total = total + (middle_[:rows] + large[rows : 2 * rows])
    return total + large[:rows]


def middle(ref, index):
    rows, group, lanes = ref.shape
    return ref.reshape(rows * group, lanes)[pl.ds(index, rows, stride=group), :]


def set_middle(ref, index, value):
    rows, group, lanes = ref.shape
    ref.reshape(rows * group, lanes)[pl.ds(index, rows, stride=group), :] = value


def project(p0, p1, p2):
    s = p1 * p1 + p2 * p2
    half = 0.5 * s
    lam = jnp.zeros_like(p0)
    for _ in range(NEWTON):
        growth = 1.0 + lam
        cube = growth * growth * growth
        lam = jnp.maximum(lam + ((p0 - lam) * cube + half * growth) / (cube + s), 0.0)
    inverse = 1.0 / (1.0 + lam)
    return p0 - lam, p1 * inverse, p2 * inverse


def kernel(
    sizes,
    mom_hbm, pot_in, rho_start, rho_end, ct_hbm, ctt_hbm, cy_hbm, cyt_hbm, et, et8, ey8,
    mom_out, pot_out,
    momv, momx, ct, ctt, cy, cyt,
    pot, ht, hyp, hwt, hwx, hwy, face_p, face_t, face_y, ht_out, wx_all, src,
    r1, s2, r2, sp, sq, s3, r3, s4, ci, cg, rip, rra,
    fwd_out, fwd_in, back_out, back_in, extra_out, extra_in,
    load_sem, halo_send, halo_recv, w_send, w_recv, th_send, th_recv, xh_send, xh_recv,
    t_send, t_recv, y_send, y_recv, p_send, p_recv, e_send, e_recv, local_sem,
):
    A, G, B, T, X, Y = sizes
    piece = X // A
    KT = NT // B
    pieces = G * A
    stages = piece // ROWS
    groups = X // ROWS
    high = ROWS * T
    ta, gx, gy = (lax.axis_index(name) for name in ("ta", "gx", "gy"))
    me = gx * A + ta
    to_t = [lax.rem(ta + d, A) for d in range(A)]
    to_x = [lax.rem(gx + d, G) for d in range(G)]
    to_y = [lax.rem(gy + d, B) for d in range(B)]
    partners = [(dx, dt) for dx in range(G) for dt in range(A)][1:]

    def remote(source, target, send, recv, where):
        return pltpu.make_async_remote_copy(
            src_ref=source, dst_ref=target, send_sem=send, recv_sem=recv,
            device_id=where, device_id_type=MESH,
        )

    loads = [
        pltpu.make_async_copy(source, target, load_sem.at[n])
        for n, (source, target) in enumerate(
            ((mom_hbm, momv), (ct_hbm, ct), (cyt_hbm, cyt), (cy_hbm, cy), (ctt_hbm, ctt))
        )
    ]
    for load in loads:
        load.start()

    barrier = pltpu.get_barrier_semaphore()
    for dx, dt in partners:
        pl.semaphore_signal(
            barrier, inc=1, device_id=(to_t[dt], to_x[dx], gy), device_id_type=MESH
        )
    for d in range(1, B):
        pl.semaphore_signal(
            barrier, inc=1, device_id=(ta, gx, to_y[d]), device_id_type=MESH
        )

    sub = lax.broadcasted_iota(jnp.int32, (high, Y), 0)
    lane = lax.broadcasted_iota(jnp.int32, (high, Y), 1)
    eye = sub == lane
    time = lax.rem(sub, T)
    low = lax.broadcasted_iota(jnp.int32, (8, 128), 0) < 4

    def pack(column):
        spread = jnp.broadcast_to(column, (high, Y))
        return jnp.sum(jnp.where(eye, spread, 0.0), axis=0, keepdims=True)

    def unpack(row):
        spread = jnp.broadcast_to(row, (high, Y))
        return jnp.sum(jnp.where(eye, spread, 0.0), axis=1, keepdims=True)

    def rows_of(parts):
        return jnp.concatenate([jnp.broadcast_to(p, (T, Y)) for p in parts], axis=0)

    def pack_first(it, n):
        value = pot[it, pl.ds(n * ROWS, ROWS), :, :].reshape(high, Y)
        face_p[it, pl.ds(n, 1), :] = pack(value[:, 0:1])

    def first(n, _):
        for r in range(ROWS):
            pot[0, n * ROWS + r] = middle(pot_in, n * ROWS + r)
        pack_first(0, n)
        return 0

    lax.fori_loop(0, groups, first, 0)
    pl.semaphore_wait(barrier, pieces + B - 2)

    def prepare():
        def coefficients(j, _):
            sigma = et[pl.ds(gy * KT, KT), :] + ey8[j][0:1, :]
            lanes = pl.ds(pl.multiple_of(j * 128, 128), 128)
            g = jnp.where(me == 0, 0.0, jnp.ones_like(sigma))
            h = sigma
            for i in range(piece - 1):
                inv = 1.0 / (g + 1.0 + h)
                g = g * inv
                ci[i, :, lanes] = inv
                cg[i, :, lanes] = g
                h = sigma + h * inv
            return 0

        lax.fori_loop(0, NY // 128, coefficients, 0)

        sigma = et8[gy * (KT // 4) + me // B] + ey8[lax.rem(me, B)]
        one = jnp.ones_like(sigma)

        def inner(i, state):
            g, h, h_first, ground = state
            inv = 1.0 / (g + 1.0 + h)
            inv_first = 1.0 / (1.0 + h_first)
            return (
                g * inv, sigma + h * inv, sigma + h_first * inv_first, ground + g * h * inv
            )

        link, h_end, h_first, ground = lax.fori_loop(
            0, piece - 1, inner, (one, sigma, sigma, jnp.zeros_like(sigma))
        )

        def outer(j, s):
            inv = 1.0 / (s + link)
            rip[j] = inv
            rra[j] = link * inv
            return jnp.where(j == pieces - 2, h_end, h_end + ground) + link * s * inv

        s_last = lax.fori_loop(0, pieces - 1, outer, h_first + ground)
        rip[pieces - 1] = jnp.where(
            s_last > 0.0, 1.0 / jnp.where(s_last > 0.0, s_last, 1.0), 0.0
        )

    def exchange(it, way, c, own, others, sends, recvs):
        local = pltpu.make_async_copy(*own, local_sem.at[it, way, c])
        local.start()
        copies = [
            remote(source, target, sends.at[it, way // 2, c, k], recvs.at[it, way // 2, c, k], where)
            for k, (source, target, where) in enumerate(others)
        ]
        for copy in copies:
            copy.start()
        return local, copies

    def along_t(it, way, c, source, target):
        return exchange(
            it, way, c, (source(ta), target),
            [(source(to_t[d]), target, (to_t[d], gx, gy)) for d in range(1, A)],
            t_send, t_recv,
        )

    def along_y(it, way, c, source, target):
        return exchange(
            it, way, c, (source(gy), target),
            [(source(to_y[d]), target, (ta, gx, to_y[d])) for d in range(1, B)],
            y_send, y_recv,
        )

    def landed(pair):
        pair[0].wait()
        for copy in pair[1]:
            copy.wait_recv()

    def sent(pairs):
        for pair in pairs:
            for copy in pair[1]:
                copy.wait_send()

    def place(i):
        return (i + piece - 1) % piece

    ends = [ROWS * (j + 1) - 1 for j in range(stages - 1)] + [piece]
    cuts = list(zip([0] + ends[:-1], ends))

    halo = [
        remote(pot_in.at[0], ht.at[0], halo_send.at[0, 0], halo_recv.at[0, 0], (to_t[A - 1], gx, gy)),
        remote(pot.at[0, 0], pot.at[0, X], halo_send.at[0, 1], halo_recv.at[0, 1], (ta, to_x[G - 1], gy)),
    ]
    for copy in halo:
        copy.start()
    t_halo, x_halo = [halo[0]], halo[1]
    unsent = []

    for it in range(ITERS):
        y_halo = remote(
            face_p.at[it], hyp.at[it], halo_send.at[it, 2], halo_recv.at[it, 2],
            (ta, gx, to_y[B - 1]),
        )
        y_halo.start()
        if it == 0:
            prepare()
            loads[0].wait()
        for copy in t_halo:
            copy.wait_recv()
        y_halo.wait_recv()

        def project_rows(j):
            def group(a, _):
                n = a * stages + j
                x = n * ROWS
                here = pot[it, pl.ds(x, ROWS), :, :].reshape(high, Y)
                nxt = rows_of([ht[it, pl.ds(x + r, 1), :] for r in range(ROWS)])
                nxt = jnp.where(time == T - 1, nxt, pltpu.roll(here, high - 1, 0))
                edge_t = (time == T - 1) & (ta == A - 1)
                slope_t = jnp.where(edge_t, 0.0, nxt - here)
                nxt = pot[it, pl.ds(x + 1, ROWS), :, :].reshape(high, Y)
                edge_x = (sub >= high - T) & ((n == groups - 1) & (gx == G - 1))
                slope_x = jnp.where(edge_x, 0.0, nxt - here)
                nxt = jnp.where(
                    lane == Y - 1, unpack(hyp[it, pl.ds(n, 1), :]), pltpu.roll(here, Y - 1, 1)
                )
                edge_y = (lane == Y - 1) & (gy == B - 1)
                slope_y = jnp.where(edge_y, 0.0, nxt - here)
                if it == 0:
                    m = [
                        jnp.concatenate(
                            [middle(momv.at[b], x + r) for r in range(ROWS)], axis=0
                        )
                        for b in range(3)
                    ]
                else:
                    m = [momx[b, pl.ds(x, ROWS), :, :].reshape(high, Y) for b in range(3)]
                q = project(slope_t + m[0], slope_x + m[1], slope_y + m[2])
                m = [old + (s - new) for old, s, new in zip(m, (slope_t, slope_x, slope_y), q)]
                for b in range(3):
                    if it == ITERS - 1:
                        for r in range(ROWS):
                            set_middle(momv.at[b], x + r, m[b][r * T : (r + 1) * T])
                    else:
                        momx[b, pl.ds(x, ROWS), :, :] = m[b].reshape(ROWS, T, Y)
                wt = jnp.where(edge_t, 0.0, m[0] - q[0])
                wx = jnp.where(edge_x, 0.0, m[1] - q[1])
                wy = jnp.where(edge_y, 0.0, m[2] - q[2])
                for r in range(ROWS):
                    face_t[j, pl.ds(a * ROWS + r, 1), :] = wt[(r + 1) * T - 1 : (r + 1) * T]
                face_y[j, pl.ds(a, 1), :] = pack(wy[:, Y - 1 : Y])
                wx_all[pl.ds(x, ROWS), :, :] = wx.reshape(ROWS, T, Y)
                last = rows_of([rho_end[pl.ds(x + r, 1), :] for r in range(ROWS)])
                begin = rows_of([rho_start[pl.ds(x + r, 1), :] for r in range(ROWS)])
                bound = jnp.where(edge_t, last, 0.0) - jnp.where(
                    (time == 0) & (ta == 0), begin, 0.0
                )
                wt_back = jnp.where(time == 0, 0.0, pltpu.roll(wt, 1, 0))
                wy_back = jnp.where(lane == 0, 0.0, pltpu.roll(wy, 1, 1))
                value = wt - wt_back + wx + (wy - wy_back) + bound
                for r in range(ROWS):
                    src[a, place(j * ROWS + r)] = value[r * T : (r + 1) * T]
                return 0

            lax.fori_loop(0, A, group, 0)

        def send_faces(j):
            copies = [
                remote(face_t.at[j], hwt.at[it, j], w_send.at[it, j, 0], w_recv.at[it, j, 0], (to_t[1], gx, gy)),
                remote(face_y.at[j], hwy.at[it, j], w_send.at[it, j, 1], w_recv.at[it, j, 1], (ta, gx, to_y[1])),
            ]
            for copy in copies:
                copy.start()
            return copies

        def finish_rows(j):
            def group(a, _):
                x = (a * stages + j) * ROWS
                before = unpack(hwy[it, j, pl.ds(a, 1), :])
                before = jnp.where((lane == 0) & (gy > 0), before, 0.0)
                early = rows_of([hwt[it, j, pl.ds(a * ROWS + r, 1), :] for r in range(ROWS)])
                before = before + jnp.where((time == 0) & (ta > 0), early, 0.0)
                for r in range(ROWS):
                    value = src[a, place(j * ROWS + r)] - before[r * T : (r + 1) * T]
                    if j + r:
                        value = value - wx_all[x + r - 1]
                    src[a, place(j * ROWS + r)] = value
                return 0

            lax.fori_loop(0, A, group, 0)

        faces, t_out = [], []

        def close_stage(j):
            for copy in faces[j]:
                copy.wait_recv()
            finish_rows(j)
            if j == stages - 1:
                wx_halo.wait_recv()
                src[0, place(0)] = src[0, place(0)] - jnp.where(gx > 0, hwx[it], 0.0)
                for a in range(1, A):
                    src[a, place(0)] = src[a, place(0)] - wx_all[a * piece - 1]
            lo, hi = cuts[j]
            t_out.append(
                along_t(
                    it, 0, j,
                    lambda other: src.at[other, pl.ds(lo, hi - lo), :, :],
                    r1.at[it, pl.ds(lo, hi - lo), pl.ds(ta * T, T), :],
                )
            )

        for j in range(stages):
            if j == stages - 1:
                x_halo.wait_recv()
            project_rows(j)
            faces.append(send_faces(j))
            if j == stages - 1:
                wx_halo = remote(
                    wx_all.at[X - 1], hwx.at[it], halo_send.at[it, 3], halo_recv.at[it, 3],
                    (ta, to_x[1], gy),
                )
                wx_halo.start()
            if j:
                close_stage(j - 1)
        close_stage(stages - 1)
        if it == ITERS - 1:
            store = pltpu.make_async_copy(momv, mom_out, load_sem.at[0])
            store.start()
        sent(unsent)
        if it == 0:
            loads[1].wait()
            loads[2].wait()

        y_out = []
        half = cuts[stages // 2 - 1][1] if stages > 1 else piece
        for j, (lo, hi) in enumerate(cuts):
            landed(t_out[j])
            for a in range(lo, hi, 2):
                some = range(a, min(a + 2, hi))
                wide = jnp.concatenate([r1[it, p] for p in some], axis=1)
                wide = table_left(ct, wide)
                for n, p in enumerate(some):
                    s2[p] = wide[:, n * Y : (n + 1) * Y]
            y_out.append(
                along_y(
                    it, 1, j,
                    lambda other: s2.at[pl.ds(lo, hi - lo), pl.ds(other * KT, KT), :],
                    r2.at[it, pl.ds(lo, hi - lo), :, pl.ds(pl.multiple_of(gy * Y, Y), Y)],
                )
            )

        def forward_y(lo, hi):
            for j in range(stages):
                if lo < cuts[j][1] <= hi:
                    landed(y_out[j])
            value = r2[it, pl.ds(lo, hi - lo), :, :].reshape((hi - lo) * KT, NY)
            value = table_right(value, cyt)
            sp[pl.ds(lo, hi - lo)] = value.reshape(hi - lo, KT, NY)

        forward_y(0, half)
        if half < piece:
            forward_y(half, piece)

        def forward(j, _):
            lanes = pl.ds(pl.multiple_of(j * 128, 128), 128)
            value = sp[place(0), :, lanes]
            left = jnp.zeros_like(value)
            for i in range(piece - 1):
                left = left + cg[i, :, lanes] * value
                value = sp[place(i + 1), :, lanes] + ci[i, :, lanes] * value
                sp[place(i + 1), :, lanes] = value
            for q in range(KT // 4):
                part = slice(8 * (q // 2), 8 * (q // 2) + 8)
                a, b = left[part], value[part]
                if q % 2:
                    tile = jnp.where(low, pltpu.roll(a, 4, 0), b)
                else:
                    tile = jnp.where(low, a, pltpu.roll(b, 4, 0))
                fwd_out[q * B + j] = tile
            return 0

        inner_sum = jnp.zeros((8, 128), jnp.float32)
        for i in range(piece - 1):
            begin = 0.5 * (piece * (piece - 1) - i * (i + 1))
            other = 0.5 * (i + 1) * (piece - 1 - i)
            inner_sum = inner_sum + jnp.where(me == 0, begin, other) * sp[place(i), 0:8, 0:128]
        extra_out[0] = inner_sum
        lax.fori_loop(0, NY // 128, forward, 0)

        def scatter(phase, outgoing, incoming):
            copies = [
                remote(
                    outgoing.at[to_x[dx] * A + to_t[dt]], incoming.at[it, me],
                    p_send.at[it, phase, n], p_recv.at[it, phase, n],
                    (to_t[dt], to_x[dx], gy),
                )
                for n, (dx, dt) in enumerate(partners)
            ]
            for copy in copies:
                copy.start()
            incoming[it, me] = outgoing[me]
            return copies

        def gather_copy(k):
            return remote(
                extra_out.at[0], extra_in.at[it, k], e_send.at[it, k], e_recv.at[it, k],
                (0, 0, gy),
            )

        def spread_copy(k):
            return remote(
                extra_out.at[1], extra_in.at[it, pieces], e_send.at[it, k], e_recv.at[it, pieces],
                (lax.rem(k, A), k // A, gy),
            )

        head = (gy == 0) & (me == 0)
        tail = (gy == 0) & (me > 0)
        gathers = scatter(0, fwd_out, fwd_in)

        @pl.when(tail)
        def _():
            gather_copy(me).start()

        @pl.when(head)
        def _():
            extra_in[it, 0] = extra_out[0]

            @pl.loop(1, pieces)
            def _(k):
                gather_copy(k).wait_recv()

        for copy in gathers:
            copy.wait_recv()

        value = fwd_in[it, 0] + pltpu.roll(fwd_in[it, 1], 4, 0)
        before = [value]
        for j in range(1, pieces):
            given = fwd_in[it, j]
            if j + 1 < pieces:
                given = given + pltpu.roll(fwd_in[it, j + 1], 4, 0)
            value = given + rra[j - 1] * value
            before.append(value)
        full = value
        value = rip[pieces - 1] * value
        weighted = value * (0.5 * (piece + 1))
        for j in range(pieces - 2, -1, -1):
            here = rip[j] * before[j] + rra[j] * value
            back_out[j + 1] = jnp.where(low, pltpu.roll(here, 4, 0), value)
            value = here
            weighted = weighted + value * (
                piece + 0.5 * (piece - 1) if j == 0 else 1.0 * piece
            )
        back_out[0] = jnp.where(low, 0.0, value)
        returns = scatter(1, back_out, back_in)

        @pl.when(head)
        def _():
            total = lax.fori_loop(
                1, pieces, lambda k, acc: acc + extra_in[it, k], extra_in[it, 0]
            )
            excess = pltpu.roll(full, 4, 0)
            level = -(total + pltpu.roll(weighted, 4, 0)) / NX - excess * (
                (NX * NX - 1.0) / (6.0 * NX)
            )
            row = lax.broadcasted_iota(jnp.int32, (8, 128), 0)
            extra_out[1] = jnp.where(row == 0, excess, pltpu.roll(level, 1, 0))
            extra_in[it, pieces] = extra_out[1]

            @pl.loop(1, pieces)
            def _(k):
                spread_copy(k).start()

        if it == 0:
            loads[3].wait()
            loads[4].wait()
        for copy in returns:
            copy.wait_recv()

        @pl.when(tail)
        def _():
            spread_copy(me).wait_recv()

        def backward(j, _):
            lanes = pl.ds(pl.multiple_of(j * 128, 128), 128)
            left, value = [], []
            for n in range(KT // 8):
                a = back_in[it, 2 * n * B + j]
                b = back_in[it, (2 * n + 1) * B + j]
                left.append(jnp.where(low, a, pltpu.roll(b, 4, 0)))
                value.append(jnp.where(low, pltpu.roll(a, 4, 0), b))
            left = jnp.concatenate(left, axis=0)
            value = jnp.concatenate(value, axis=0)
            sq[piece - 1, :, lanes] = value
            for i in range(piece - 2, -1, -1):
                value = (
                    ci[i, :, lanes] * (sp[place(i), :, lanes] + value)
                    + cg[i, :, lanes] * left
                )
                sq[i, :, lanes] = value
            return 0

        lax.fori_loop(0, NY // 128, backward, 0)

        @pl.when(gy == 0)
        def _():
            row = lax.broadcasted_iota(jnp.int32, (8, 128), 0)
            constant = (row == 0) & (lax.broadcasted_iota(jnp.int32, (8, 128), 1) == 0)
            excess = extra_in[it, pieces]
            level = pltpu.roll(excess, 7, 0)
            for i in range(piece):
                cell = (me * piece + i).astype(jnp.float32)
                ramp = cell * (cell + 1.0) * (0.5 / NX)
                sq[i, 0:8, 0:128] += jnp.where(constant, excess * ramp + level, 0.0)

        y_back, t_back = [], []
        parts = 2 if stages % 2 == 0 else 1
        for n in range(parts):
            count = piece // parts
            lines = pl.ds(n * count, count)
            value = table_right(sq[lines].reshape(count * KT, NY), cy)
            s3[lines] = value.reshape(count, KT, NY)
            for j in range(n * stages // parts, (n + 1) * stages // parts):
                y_back.append(
                    along_y(
                        it, 3, j,
                        lambda other: s3.at[
                            pl.ds(j * ROWS, ROWS), :, pl.ds(pl.multiple_of(other * Y, Y), Y)
                        ],
                        r3.at[it, pl.ds(j * ROWS, ROWS), pl.ds(gy * KT, KT), :],
                    )
                )
        more = it + 1 < ITERS

        def x_copy(d):
            return remote(
                s4.at[0, pl.ds(d * T, T), :], pot.at[it + 1, X],
                xh_send.at[it, d], xh_recv.at[it], (d, to_x[G - 1], gy),
            )

        for j in range(stages):
            landed(y_back[j])
            for x in range(j * ROWS, (j + 1) * ROWS, 2):
                wide = jnp.concatenate([r3[it, x], r3[it, x + 1]], axis=1)
                wide = table_left(ctt, wide)
                for n in range(2):
                    value = wide[:, n * Y : (n + 1) * Y]
                    s4[x + n] = value
                    if more:
                        for d in range(A):
                            t = (d + 1) * T % NT
                            ht_out[d, x + n : x + n + 1, :] = value[t : t + 1]
            if more and j == stages - 1:
                ht[it + 1, pl.ds(ta * piece, piece), :] = ht_out[ta]
                t_halo = [
                    remote(
                        ht_out.at[to_t[d]], ht.at[it + 1, pl.ds(ta * piece, piece), :],
                        th_send.at[it, d - 1], th_recv.at[it, d - 1], (to_t[d], gx, gy),
                    )
                    for d in range(1, A)
                ]
                for copy in t_halo:
                    copy.start()
            t_back.append(
                along_t(
                    it, 2, j,
                    lambda other: s4.at[pl.ds(j * ROWS, ROWS), pl.ds(other * T, T), :],
                    pot.at[it + 1, pl.ds(ta * piece + j * ROWS, ROWS), :, :],
                )
            )
            if more and j == 0:

                @pl.when(ta == 0)
                def _():
                    for d in range(A):
                        x_copy(d).start()

        for j in range(stages):
            landed(t_back[j])

            def arrived(a, _):
                n = a * stages + j
                if more:
                    pack_first(it + 1, n)
                else:
                    for r in range(ROWS):
                        set_middle(pot_out, n * ROWS + r, pot[it + 1, n * ROWS + r])
                return 0

            lax.fori_loop(0, A, arrived, 0)

        if it == 0:
            for copy in halo:
                copy.wait_send()
        y_halo.wait_send()
        wx_halo.wait_send()
        for copies in faces:
            for copy in copies:
                copy.wait_send()
        sent(t_out + y_out + y_back)
        for copy in gathers + returns:
            copy.wait_send()

        @pl.when(tail)
        def _():
            gather_copy(me).wait_send()

        @pl.when(head)
        def _():
            @pl.loop(1, pieces)
            def _(k):
                spread_copy(k).wait_send()

        sent(t_back)
        if more:
            x_halo = x_copy(0)
            for copy in t_halo:
                copy.wait_send()

            @pl.when(ta == 0)
            def _():
                for d in range(A):
                    x_copy(d).wait_send()

    store.wait()


def parts_of(table):
    parts, rest = [], np.asarray(table, np.float64)
    for _ in range(3):
        part = rest.astype(np.float32).astype(jnp.bfloat16)
        parts.append(part)
        rest = rest - part.astype(np.float64)
    return np.stack(parts)


def on_device(sizes, momenta, potential, rho_start, rho_end):
    A, G, B, T, X, Y = sizes
    piece, KT, pieces = X // A, NT // B, G * A
    stages, groups = piece // ROWS, X // ROWS
    assert Y == 128 and ROWS * T <= 128 and T % 8 == 0 and piece % ROWS == 0
    assert KT % 8 == 0 and pieces == (KT // 4) * B and ITERS > 1
    table_t, table_y = parts_of(cosine_table(NT)), parts_of(cosine_table(NY))
    turned_t, turned_y = parts_of(cosine_table(NT).T), parts_of(cosine_table(NY).T)
    e_t = eigenvalue(NT)
    spread_t = np.broadcast_to(e_t[:, None], (NT, 128)).astype(np.float32)
    spread_8 = np.broadcast_to(
        np.concatenate([e_t.reshape(NT // 4, 4)] * 2, axis=1)[:, :, None], (NT // 4, 8, 128)
    ).astype(np.float32)
    spread_y = np.broadcast_to(
        eigenvalue(NY).reshape(B, 1, 128), (B, 8, 128)
    ).astype(np.float32)
    tables = [
        table_t.reshape(3 * NT, NT), turned_t.reshape(3 * NT, NT), table_y, turned_y,
        spread_t, spread_8, spread_y,
    ]
    operands = [momenta, potential, rho_start, rho_end] + [
        jnp.asarray(np.ascontiguousarray(table)) for table in tables
    ]
    f32 = jnp.float32
    vmem = pl.BlockSpec(memory_space=pltpu.VMEM)
    hbm = pl.BlockSpec(memory_space=pl.ANY)
    dma = pltpu.SemaphoreType.DMA
    tall = max(groups, 8)

    def held(*shape, dtype=f32):
        return pltpu.VMEM(shape, dtype)

    return pl.pallas_call(
        functools.partial(kernel, sizes),
        out_shape=(
            jax.ShapeDtypeStruct(momenta.shape, f32),
            jax.ShapeDtypeStruct(potential.shape, f32),
        ),
        in_specs=[hbm, vmem, vmem, vmem, hbm, hbm, hbm, hbm, vmem, vmem, vmem],
        out_specs=(hbm, vmem),
        scratch_shapes=[
            held(3, T, X, Y),
            held(3, X, T, Y),
            held(3 * NT, NT, dtype=jnp.bfloat16),
            held(3 * NT, NT, dtype=jnp.bfloat16),
            held(3, NY, NY, dtype=jnp.bfloat16),
            held(3, NY, NY, dtype=jnp.bfloat16),
            held(ITERS + 1, X + 1, T, Y),
            held(ITERS, X, Y),
            held(ITERS, tall, Y),
            held(ITERS, stages, A * ROWS, Y),
            held(ITERS, T, Y),
            held(ITERS, stages, 8, Y),
            held(ITERS, tall, Y),
            held(stages, A * ROWS, Y),
            held(stages, 8, Y),
            held(A, piece, Y),
            held(X, T, Y),
            held(A, piece, T, Y),
            held(ITERS, piece, NT, Y),
            held(piece, NT, Y),
            held(ITERS, piece, KT, NY),
            held(piece, KT, NY),
            held(piece, KT, NY),
            held(piece, KT, NY),
            held(ITERS, piece, NT, Y),
            held(piece, NT, Y),
            held(piece, KT, NY),
            held(piece, KT, NY),
            held(pieces, 8, 128),
            held(pieces, 8, 128),
            held(pieces, 8, 128),
            held(ITERS, pieces, 8, 128),
            held(pieces, 8, 128),
            held(ITERS, pieces, 8, 128),
            held(2, 8, 128),
            held(ITERS, pieces + 1, 8, 128),
            dma((5,)),
            dma((ITERS, 4)),
            dma((ITERS, 4)),
            dma((ITERS, stages, 2)),
            dma((ITERS, stages, 2)),
            dma((ITERS, A - 1)),
            dma((ITERS, A - 1)),
            dma((ITERS, A)),
            dma((ITERS,)),
            dma((ITERS, 2, stages, A - 1)),
            dma((ITERS, 2, stages, A - 1)),
            dma((ITERS, 2, stages, B - 1)),
            dma((ITERS, 2, stages, B - 1)),
            dma((ITERS, 2, pieces - 1)),
            dma((ITERS, 2, pieces - 1)),
            dma((ITERS, pieces)),
            dma((ITERS, pieces + 1)),
            dma((ITERS, 4, stages)),
        ],
        compiler_params=pltpu.CompilerParams(
            collective_id=0, has_side_effects=True, vmem_limit_bytes=60 << 20
        ),
    )(*operands)


def solution(mesh):
    A, G, B = (mesh.shape[name] for name in ("ta", "gx", "gy"))
    sizes = (A, G, B, NT // A, NX // G, NY // B)
    placed = (P(None, "ta", "gx", "gy"), P("ta", "gx", "gy"), P("gx", "gy"), P("gx", "gy"))
    return jax.shard_map(
        functools.partial(on_device, sizes),
        mesh=mesh,
        in_specs=placed,
        out_specs=(P(None, "ta", "gx", "gy"), P("ta", "gx", "gy")),
        check_vma=False,
    )
```

time: 243 us -> 205 us (0.84)
  Pallas kernels: 237 us -> 199 us
    pallas_call x1, Pallas kernels: 237 us -> 199 us  [on_device(): pl.pallas_call(functools.partial(kernel, sizes), out_shape=(jax.ShapeDtyp...]
where the time goes in v3:
time: 205 us
  Pallas kernels  199 us (97%)
  local copies, waits for them, and re-layouts  5.03 us (2%)
    pallas_call x1, Pallas kernels, on_device(): pl.pallas_call(functools.partial(kernel, sizes), out_shape=(jax.ShapeDtyp...  199 us
    unnamed x4, local copies, waits for them, and re-layouts  5.03 us

profile of v3, /device:TPU:1, one launch (start us, length us, event | category | flops | bytes accessed | tf_op | source)
XLA Modules:
  0.0 205.0 jit_solution(11473106188717153975)
XLA Ops:
  0.6 199.3 %shard_map.122 = (f32[3,32,64,128]{3,2,1,0:T(8,128)}, f32[32,64,128]{2,1,0:T(8,128)}) custom-call(f32[3,32,64,128]{3,2,1,0:T(8,128)} %mom_hbm.1, f32[32,64,128]{2,1,0:T(8,128)} %pot_in.1, f32[64,128]{1,0:T(8,128)} %rho_start.1, f32[64,128]{1,0:T(8,128)} %rho_end.1, bf16[384,128]{1,0:T(8,128)(2,1)} %constant.14.clone.ct_hbm, ...), custom_call_target="tpu_custom_call" | custom-call | tf_op jit(solution)/shard_map/pallas_call | solution.py:731
  199.9 0.0 copy-start
  199.9 4.1 %copy.15 = f32[3,32,64,128]{3,2,1,0:T(8,128)} copy(f32[3,32,64,128]{3,2,1,0:T(8,128)} %get-tuple-element.4) | data formatting | bytes 6291456
  204.0 0.0 copy-done
  204.0 1.0 copy.16
Async XLA Ops:
  199.9 4.1 %copy-start = (f32[32,64,128]{2,1,0:T(8,128)S(1)}, f32[32,64,128]{2,1,0:T(8,128)}, u32[]{:S(2)}) copy-start(f32[32,64,128]{2,1,0:T(8,128)} %get-tuple-element.5) | copy-start | bytes 3145732

commit v4 on v3

--- a/solution.py
+++ b/solution.py
@@ -95,7 +95,8 @@
     pot, ht, hyp, hwt, hwx, hwy, face_p, face_t, face_y, ht_out, wx_all, src,
     r1, s2, r2, sp, sq, s3, r3, s4, ci, cg, rip, rra,
     fwd_out, fwd_in, back_out, back_in, extra_out, extra_in,
-    load_sem, halo_send, halo_recv, w_send, w_recv, th_send, th_recv, xh_send, xh_recv,
+    load_sem, halo_send, halo_recv, yh_send, yh_recv, w_send, w_recv, wx_send, wx_recv,
+    th_send, th_recv, xh_send, xh_recv,
     t_send, t_recv, y_send, y_recv, p_send, p_recv, e_send, e_recv, local_sem,
 ):
     A, G, B, T, X, Y = sizes
@@ -110,7 +111,10 @@
     to_t = [lax.rem(ta + d, A) for d in range(A)]
     to_x = [lax.rem(gx + d, G) for d in range(G)]
     to_y = [lax.rem(gy + d, B) for d in range(B)]
-    partners = [(dx, dt) for dx in range(G) for dt in range(A)][1:]
+    partners = sorted(
+        ((dx, dt) for dx in range(G) for dt in range(A) if dx or dt),
+        key=lambda p: -(4 * (p[0] % 2) + min(p[0], G - p[0]) + min(p[1], A - p[1])),
+    )
 
     def remote(source, target, send, recv, where):
         return pltpu.make_async_remote_copy(
@@ -154,17 +158,26 @@
     def rows_of(parts):
         return jnp.concatenate([jnp.broadcast_to(p, (T, Y)) for p in parts], axis=0)
 
-    def pack_first(it, n):
-        value = pot[it, pl.ds(n * ROWS, ROWS), :, :].reshape(high, Y)
-        face_p[it, pl.ds(n, 1), :] = pack(value[:, 0:1])
-
-    def first(n, _):
-        for r in range(ROWS):
-            pot[0, n * ROWS + r] = middle(pot_in, n * ROWS + r)
-        pack_first(0, n)
+    def pack_first(it, j):
+        def group(a, _):
+            x = (a * stages + j) * ROWS
+            value = pot[it, pl.ds(x, ROWS), :, :].reshape(high, Y)
+            face_p[it, j, pl.ds(a, 1), :] = pack(value[:, 0:1])
+            return 0
+
+        lax.fori_loop(0, A, group, 0)
+
+    def first(a, _):
+        for j in range(stages):
+            for r in range(ROWS):
+                x = (a * stages + j) * ROWS + r
+                pot[0, x] = middle(pot_in, x)
+                ht_out[j, a, r : r + 1, :] = pot_in[0, pl.ds(x, 1), :]
         return 0
 
-    lax.fori_loop(0, groups, first, 0)
+    lax.fori_loop(0, A, first, 0)
+    for j in range(stages):
+        pack_first(0, j)
     pl.semaphore_wait(barrier, pieces + B - 2)
 
     def prepare():
@@ -247,157 +260,184 @@
     def place(i):
         return (i + piece - 1) % piece
 
-    ends = [ROWS * (j + 1) - 1 for j in range(stages - 1)] + [piece]
-    cuts = list(zip([0] + ends[:-1], ends))
+    done = [ROWS * (j + 1) - 1 for j in range(stages)]
+    cuts = [(j, ROWS * j - 1 if j else 0, done[j]) for j in range(stages - 1)]
+    cuts += [(stages - 1, ROWS * (stages - 1) - 1, piece - 2), (stages - 1, piece - 2, piece)]
+    marks = [0, 2] + list(range(5, piece, 3))[: 2 if stages > 2 else 0]
+    marks += list(range(marks[-1] + ROWS, piece, ROWS)) + [piece]
+    backs = list(zip(marks[:-1], marks[1:]))
+
+    def y_face(it, j):
+        return remote(
+            face_p.at[it, j], hyp.at[it, j], yh_send.at[it, j], yh_recv.at[it, j],
+            (ta, gx, to_y[B - 1]),
+        )
+
+    def t_face(it, j, d):
+        return remote(
+            ht_out.at[j, to_t[d]], ht.at[it + 1, j, ta], th_send.at[it, j, d - 1],
+            th_recv.at[it, j, d - 1], (to_t[d], gx, gy),
+        )
+
+    def x_face(it, d):
+        return remote(
+            s4.at[0, pl.ds(d * T, T), :], pot.at[it + 1, X],
+            xh_send.at[it, d], xh_recv.at[it], (d, to_x[G - 1], gy),
+        )
+
+    def wx_face(it):
+        return remote(
+            wx_all.at[X - 1], hwx.at[it], wx_send.at[it], wx_recv.at[it], (ta, to_x[1], gy)
+        )
 
     halo = [
-        remote(pot_in.at[0], ht.at[0], halo_send.at[0, 0], halo_recv.at[0, 0], (to_t[A - 1], gx, gy)),
-        remote(pot.at[0, 0], pot.at[0, X], halo_send.at[0, 1], halo_recv.at[0, 1], (ta, to_x[G - 1], gy)),
+        remote(ht_out, ht.at[0], halo_send.at[0], halo_recv.at[0], (to_t[A - 1], gx, gy)),
+        remote(pot.at[0, 0], pot.at[0, X], halo_send.at[1], halo_recv.at[1], (ta, to_x[G - 1], gy)),
     ]
+    for j in range(stages):
+        y_face(0, j).start()
     for copy in halo:
         copy.start()
-    t_halo, x_halo = [halo[0]], halo[1]
+    faces = [[] for _ in range(ITERS)]
+    t_out = [[] for _ in range(ITERS)]
     unsent = []
 
+    def project_rows(it, j):
+        def group(a, _):
+            n = a * stages + j
+            x = n * ROWS
+            here = pot[it, pl.ds(x, ROWS), :, :].reshape(high, Y)
+            nxt = rows_of([ht[it, j, a, r : r + 1, :] for r in range(ROWS)])
+            nxt = jnp.where(time == T - 1, nxt, pltpu.roll(here, high - 1, 0))
+            edge_t = (time == T - 1) & (ta == A - 1)
+            slope_t = jnp.where(edge_t, 0.0, nxt - here)
+            nxt = pot[it, pl.ds(x + 1, ROWS), :, :].reshape(high, Y)
+            edge_x = (sub >= high - T) & ((n == groups - 1) & (gx == G - 1))
+            slope_x = jnp.where(edge_x, 0.0, nxt - here)
+            nxt = jnp.where(
+                lane == Y - 1, unpack(hyp[it, j, pl.ds(a, 1), :]), pltpu.roll(here, Y - 1, 1)
+            )
+            edge_y = (lane == Y - 1) & (gy == B - 1)
+            slope_y = jnp.where(edge_y, 0.0, nxt - here)
+            if it == 0:
+                m = [
+                    jnp.concatenate(
+                        [middle(momv.at[b], x + r) for r in range(ROWS)], axis=0
+                    )
+                    for b in range(3)
+                ]
+            else:
+                m = [momx[b, pl.ds(x, ROWS), :, :].reshape(high, Y) for b in range(3)]
+            q = project(slope_t + m[0], slope_x + m[1], slope_y + m[2])
+            m = [old + (s - new) for old, s, new in zip(m, (slope_t, slope_x, slope_y), q)]
+            for b in range(3):
+                if it == ITERS - 1:
+                    for r in range(ROWS):
+                        set_middle(momv.at[b], x + r, m[b][r * T : (r + 1) * T])
+                else:
+                    momx[b, pl.ds(x, ROWS), :, :] = m[b].reshape(ROWS, T, Y)
+            wt = jnp.where(edge_t, 0.0, m[0] - q[0])
+            wx = jnp.where(edge_x, 0.0, m[1] - q[1])
+            wy = jnp.where(edge_y, 0.0, m[2] - q[2])
+            for r in range(ROWS):
+                face_t[j, pl.ds(a * ROWS + r, 1), :] = wt[(r + 1) * T - 1 : (r + 1) * T]
+            face_y[j, pl.ds(a, 1), :] = pack(wy[:, Y - 1 : Y])
+            wx_all[pl.ds(x, ROWS), :, :] = wx.reshape(ROWS, T, Y)
+            last = rows_of([rho_end[pl.ds(x + r, 1), :] for r in range(ROWS)])
+            begin = rows_of([rho_start[pl.ds(x + r, 1), :] for r in range(ROWS)])
+            bound = jnp.where(edge_t, last, 0.0) - jnp.where(
+                (time == 0) & (ta == 0), begin, 0.0
+            )
+            wt_back = jnp.where(time == 0, 0.0, pltpu.roll(wt, 1, 0))
+            wy_back = jnp.where(lane == 0, 0.0, pltpu.roll(wy, 1, 1))
+            value = wt - wt_back + wx + (wy - wy_back) + bound
+            for r in range(ROWS):
+                src[a, place(j * ROWS + r)] = value[r * T : (r + 1) * T]
+            return 0
+
+        lax.fori_loop(0, A, group, 0)
+
+    def send_faces(it, j):
+        copies = [
+            remote(face_t.at[j], hwt.at[it, j], w_send.at[it, j, 0], w_recv.at[it, j, 0], (to_t[1], gx, gy)),
+            remote(face_y.at[j], hwy.at[it, j], w_send.at[it, j, 1], w_recv.at[it, j, 1], (ta, gx, to_y[1])),
+        ]
+        for copy in copies:
+            copy.start()
+        return copies
+
+    def finish_rows(it, j):
+        def group(a, _):
+            x = (a * stages + j) * ROWS
+            before = unpack(hwy[it, j, pl.ds(a, 1), :])
+            before = jnp.where((lane == 0) & (gy > 0), before, 0.0)
+            early = rows_of([hwt[it, j, pl.ds(a * ROWS + r, 1), :] for r in range(ROWS)])
+            before = before + jnp.where((time == 0) & (ta > 0), early, 0.0)
+            for r in range(ROWS):
+                value = src[a, place(j * ROWS + r)] - before[r * T : (r + 1) * T]
+                if j + r:
+                    value = value - wx_all[x + r - 1]
+                src[a, place(j * ROWS + r)] = value
+            return 0
+
+        lax.fori_loop(0, A, group, 0)
+
+    def close_stage(it, j):
+        for copy in faces[it][j]:
+            copy.wait_recv()
+        finish_rows(it, j)
+        if j == stages - 1:
+            wx_face(it).wait_recv()
+            src[0, place(0)] = src[0, place(0)] - jnp.where(gx > 0, hwx[it], 0.0)
+            for a in range(1, A):
+                src[a, place(0)] = src[a, place(0)] - wx_all[a * piece - 1]
+        for c, (stage, lo, hi) in enumerate(cuts):
+            if stage == j:
+                t_out[it].append(
+                    along_t(
+                        it, 0, c,
+                        lambda other: src.at[other, pl.ds(lo, hi - lo), :, :],
+                        r1.at[it, pl.ds(lo, hi - lo), pl.ds(ta * T, T), :],
+                    )
+                )
+
+    def run_stage(it, j):
+        if it:
+            for d in range(1, A):
+                t_face(it - 1, j, d).wait_recv()
+        y_face(it, j).wait_recv()
+        if j == stages - 1:
+            if it:
+                x_face(it - 1, 0).wait_recv()
+            else:
+                halo[1].wait_recv()
+        project_rows(it, j)
+        faces[it].append(send_faces(it, j))
+        if j == stages - 1:
+            wx_face(it).start()
+        if j:
+            close_stage(it, j - 1)
+        if j == stages - 1:
+            close_stage(it, j)
+
+    loads[0].wait()
+    halo[0].wait_recv()
+    for j in range(stages):
+        run_stage(0, j)
+    prepare()
+    loads[1].wait()
+    loads[2].wait()
+    for copy in halo:
+        copy.wait_send()
+
     for it in range(ITERS):
-        y_halo = remote(
-            face_p.at[it], hyp.at[it], halo_send.at[it, 2], halo_recv.at[it, 2],
-            (ta, gx, to_y[B - 1]),
-        )
-        y_halo.start()
-        if it == 0:
-            prepare()
-            loads[0].wait()
-        for copy in t_halo:
-            copy.wait_recv()
-        y_halo.wait_recv()
-
-        def project_rows(j):
-            def group(a, _):
-                n = a * stages + j
-                x = n * ROWS
-                here = pot[it, pl.ds(x, ROWS), :, :].reshape(high, Y)
-                nxt = rows_of([ht[it, pl.ds(x + r, 1), :] for r in range(ROWS)])
-                nxt = jnp.where(time == T - 1, nxt, pltpu.roll(here, high - 1, 0))
-                edge_t = (time == T - 1) & (ta == A - 1)
-                slope_t = jnp.where(edge_t, 0.0, nxt - here)
-                nxt = pot[it, pl.ds(x + 1, ROWS), :, :].reshape(high, Y)
-                edge_x = (sub >= high - T) & ((n == groups - 1) & (gx == G - 1))
-                slope_x = jnp.where(edge_x, 0.0, nxt - here)
-                nxt = jnp.where(
-                    lane == Y - 1, unpack(hyp[it, pl.ds(n, 1), :]), pltpu.roll(here, Y - 1, 1)
-                )
-                edge_y = (lane == Y - 1) & (gy == B - 1)
-                slope_y = jnp.where(edge_y, 0.0, nxt - here)
-                if it == 0:
-                    m = [
-                        jnp.concatenate(
-                            [middle(momv.at[b], x + r) for r in range(ROWS)], axis=0
-                        )
-                        for b in range(3)
-                    ]
-                else:
-                    m = [momx[b, pl.ds(x, ROWS), :, :].reshape(high, Y) for b in range(3)]
-                q = project(slope_t + m[0], slope_x + m[1], slope_y + m[2])
-                m = [old + (s - new) for old, s, new in zip(m, (slope_t, slope_x, slope_y), q)]
-                for b in range(3):
-                    if it == ITERS - 1:
-                        for r in range(ROWS):
-                            set_middle(momv.at[b], x + r, m[b][r * T : (r + 1) * T])
-                    else:
-                        momx[b, pl.ds(x, ROWS), :, :] = m[b].reshape(ROWS, T, Y)
-                wt = jnp.where(edge_t, 0.0, m[0] - q[0])
-                wx = jnp.where(edge_x, 0.0, m[1] - q[1])
-                wy = jnp.where(edge_y, 0.0, m[2] - q[2])
-                for r in range(ROWS):
-                    face_t[j, pl.ds(a * ROWS + r, 1), :] = wt[(r + 1) * T - 1 : (r + 1) * T]
-                face_y[j, pl.ds(a, 1), :] = pack(wy[:, Y - 1 : Y])
-                wx_all[pl.ds(x, ROWS), :, :] = wx.reshape(ROWS, T, Y)
-                last = rows_of([rho_end[pl.ds(x + r, 1), :] for r in range(ROWS)])
-                begin = rows_of([rho_start[pl.ds(x + r, 1), :] for r in range(ROWS)])
-                bound = jnp.where(edge_t, last, 0.0) - jnp.where(
-                    (time == 0) & (ta == 0), begin, 0.0
-                )
-                wt_back = jnp.where(time == 0, 0.0, pltpu.roll(wt, 1, 0))
-                wy_back = jnp.where(lane == 0, 0.0, pltpu.roll(wy, 1, 1))
-                value = wt - wt_back + wx + (wy - wy_back) + bound
-                for r in range(ROWS):
-                    src[a, place(j * ROWS + r)] = value[r * T : (r + 1) * T]
-                return 0
-
-            lax.fori_loop(0, A, group, 0)
-
-        def send_faces(j):
-            copies = [
-                remote(face_t.at[j], hwt.at[it, j], w_send.at[it, j, 0], w_recv.at[it, j, 0], (to_t[1], gx, gy)),
-                remote(face_y.at[j], hwy.at[it, j], w_send.at[it, j, 1], w_recv.at[it, j, 1], (ta, gx, to_y[1])),
-            ]
-            for copy in copies:
-                copy.start()
-            return copies
-
-        def finish_rows(j):
-            def group(a, _):
-                x = (a * stages + j) * ROWS
-                before = unpack(hwy[it, j, pl.ds(a, 1), :])
-                before = jnp.where((lane == 0) & (gy > 0), before, 0.0)
-                early = rows_of([hwt[it, j, pl.ds(a * ROWS + r, 1), :] for r in range(ROWS)])
-                before = before + jnp.where((time == 0) & (ta > 0), early, 0.0)
-                for r in range(ROWS):
-                    value = src[a, place(j * ROWS + r)] - before[r * T : (r + 1) * T]
-                    if j + r:
-                        value = value - wx_all[x + r - 1]
-                    src[a, place(j * ROWS + r)] = value
-                return 0
-
-            lax.fori_loop(0, A, group, 0)
-
-        faces, t_out = [], []
-
-        def close_stage(j):
-            for copy in faces[j]:
-                copy.wait_recv()
-            finish_rows(j)
-            if j == stages - 1:
-                wx_halo.wait_recv()
-                src[0, place(0)] = src[0, place(0)] - jnp.where(gx > 0, hwx[it], 0.0)
-                for a in range(1, A):
-                    src[a, place(0)] = src[a, place(0)] - wx_all[a * piece - 1]
-            lo, hi = cuts[j]
-            t_out.append(
-                along_t(
-                    it, 0, j,
-                    lambda other: src.at[other, pl.ds(lo, hi - lo), :, :],
-                    r1.at[it, pl.ds(lo, hi - lo), pl.ds(ta * T, T), :],
-                )
-            )
-
-        for j in range(stages):
-            if j == stages - 1:
-                x_halo.wait_recv()
-            project_rows(j)
-            faces.append(send_faces(j))
-            if j == stages - 1:
-                wx_halo = remote(
-                    wx_all.at[X - 1], hwx.at[it], halo_send.at[it, 3], halo_recv.at[it, 3],
-                    (ta, to_x[1], gy),
-                )
-                wx_halo.start()
-            if j:
-                close_stage(j - 1)
-        close_stage(stages - 1)
         if it == ITERS - 1:
             store = pltpu.make_async_copy(momv, mom_out, load_sem.at[0])
             store.start()
-        sent(unsent)
-        if it == 0:
-            loads[1].wait()
-            loads[2].wait()
 
         y_out = []
-        half = cuts[stages // 2 - 1][1] if stages > 1 else piece
-        for j, (lo, hi) in enumerate(cuts):
-            landed(t_out[j])
+        for c, (_, lo, hi) in enumerate(cuts):
+            landed(t_out[it][c])
             for a in range(lo, hi, 2):
                 some = range(a, min(a + 2, hi))
                 wide = jnp.concatenate([r1[it, p] for p in some], axis=1)
@@ -406,23 +446,23 @@
                     s2[p] = wide[:, n * Y : (n + 1) * Y]
             y_out.append(
                 along_y(
-                    it, 1, j,
+                    it, 1, c,
                     lambda other: s2.at[pl.ds(lo, hi - lo), pl.ds(other * KT, KT), :],
                     r2.at[it, pl.ds(lo, hi - lo), :, pl.ds(pl.multiple_of(gy * Y, Y), Y)],
                 )
             )
 
         def forward_y(lo, hi):
-            for j in range(stages):
-                if lo < cuts[j][1] <= hi:
-                    landed(y_out[j])
+            for c in range(len(cuts)):
+                if lo < cuts[c][2] <= hi:
+                    landed(y_out[c])
             value = r2[it, pl.ds(lo, hi - lo), :, :].reshape((hi - lo) * KT, NY)
             value = table_right(value, cyt)
             sp[pl.ds(lo, hi - lo)] = value.reshape(hi - lo, KT, NY)
 
-        forward_y(0, half)
-        if half < piece:
-            forward_y(half, piece)
+        bounds = [0, done[max(stages // 2 - 1, 0)], piece - 2, piece]
+        for lo, hi in zip(bounds[:-1], bounds[1:]):
+            forward_y(lo, hi)
 
         def forward(j, _):
             lanes = pl.ds(pl.multiple_of(j * 128, 128), 128)
@@ -576,90 +616,71 @@
                 sq[i, 0:8, 0:128] += jnp.where(constant, excess * ramp + level, 0.0)
 
         y_back, t_back = [], []
-        parts = 2 if stages % 2 == 0 else 1
-        for n in range(parts):
-            count = piece // parts
-            lines = pl.ds(n * count, count)
-            value = table_right(sq[lines].reshape(count * KT, NY), cy)
-            s3[lines] = value.reshape(count, KT, NY)
-            for j in range(n * stages // parts, (n + 1) * stages // parts):
-                y_back.append(
-                    along_y(
-                        it, 3, j,
-                        lambda other: s3.at[
-                            pl.ds(j * ROWS, ROWS), :, pl.ds(pl.multiple_of(other * Y, Y), Y)
-                        ],
-                        r3.at[it, pl.ds(j * ROWS, ROWS), pl.ds(gy * KT, KT), :],
+        bounds = [0, 2] + ([backs[2][1]] if stages > 2 else []) + [piece]
+        for lo, hi in zip(bounds[:-1], bounds[1:]):
+            value = table_right(sq[pl.ds(lo, hi - lo)].reshape((hi - lo) * KT, NY), cy)
+            s3[pl.ds(lo, hi - lo)] = value.reshape(hi - lo, KT, NY)
+            for c, (low_row, high_row) in enumerate(backs):
+                if lo <= low_row and high_row <= hi:
+                    lines = pl.ds(low_row, high_row - low_row)
+                    y_back.append(
+                        along_y(
+                            it, 3, c,
+                            lambda other: s3.at[
+                                lines, :, pl.ds(pl.multiple_of(other * Y, Y), Y)
+                            ],
+                            r3.at[it, lines, pl.ds(gy * KT, KT), :],
+                        )
                     )
-                )
         more = it + 1 < ITERS
-
-        def x_copy(d):
-            return remote(
-                s4.at[0, pl.ds(d * T, T), :], pot.at[it + 1, X],
-                xh_send.at[it, d], xh_recv.at[it], (d, to_x[G - 1], gy),
-            )
-
-        for j in range(stages):
-            landed(y_back[j])
-            for x in range(j * ROWS, (j + 1) * ROWS, 2):
-                wide = jnp.concatenate([r3[it, x], r3[it, x + 1]], axis=1)
+        sent(unsent)
+        if it:
+
+            @pl.when(ta == 0)
+            def _():
+                for d in range(A):
+                    x_face(it - 1, d).wait_send()
+
+        for c, (lo, hi) in enumerate(backs):
+            landed(y_back[c])
+            for x in range(lo, hi, 2):
+                some = range(x, min(x + 2, hi))
+                wide = jnp.concatenate([r3[it, p] for p in some], axis=1)
                 wide = table_left(ctt, wide)
-                for n in range(2):
+                for n, p in enumerate(some):
                     value = wide[:, n * Y : (n + 1) * Y]
-                    s4[x + n] = value
+                    s4[p] = value
                     if more:
                         for d in range(A):
                             t = (d + 1) * T % NT
-                            ht_out[d, x + n : x + n + 1, :] = value[t : t + 1]
-            if more and j == stages - 1:
-                ht[it + 1, pl.ds(ta * piece, piece), :] = ht_out[ta]
-                t_halo = [
-                    remote(
-                        ht_out.at[to_t[d]], ht.at[it + 1, pl.ds(ta * piece, piece), :],
-                        th_send.at[it, d - 1], th_recv.at[it, d - 1], (to_t[d], gx, gy),
-                    )
-                    for d in range(1, A)
-                ]
-                for copy in t_halo:
-                    copy.start()
+                            r = p % ROWS
+                            ht_out[p // ROWS, d, r : r + 1, :] = value[t : t + 1]
+            if more:
+                for j in range(stages):
+                    if lo < ROWS * (j + 1) <= hi:
+                        ht[it + 1, j, ta] = ht_out[j, ta]
+                        for d in range(1, A):
+                            t_face(it, j, d).start()
             t_back.append(
                 along_t(
-                    it, 2, j,
-                    lambda other: s4.at[pl.ds(j * ROWS, ROWS), pl.ds(other * T, T), :],
-                    pot.at[it + 1, pl.ds(ta * piece + j * ROWS, ROWS), :, :],
+                    it, 2, c,
+                    lambda other: s4.at[pl.ds(lo, hi - lo), pl.ds(other * T, T), :],
+                    pot.at[it + 1, pl.ds(ta * piece + lo, hi - lo), pl.ds(0, T), :],
                 )
             )
-            if more and j == 0:
+            if more and c == 0:
 
                 @pl.when(ta == 0)
                 def _():
                     for d in range(A):
-                        x_copy(d).start()
-
+                        x_face(it, d).start()
+
+        wx_face(it).wait_send()
         for j in range(stages):
-            landed(t_back[j])
-
-            def arrived(a, _):
-                n = a * stages + j
-                if more:
-                    pack_first(it + 1, n)
-                else:
-                    for r in range(ROWS):
-                        set_middle(pot_out, n * ROWS + r, pot[it + 1, n * ROWS + r])
-                return 0
-
-            lax.fori_loop(0, A, arrived, 0)
-
-        if it == 0:
-            for copy in halo:
+            y_face(it, j).wait_send()
+            for copy in faces[it][j]:
                 copy.wait_send()
-        y_halo.wait_send()
-        wx_halo.wait_send()
-        for copies in faces:
-            for copy in copies:
-                copy.wait_send()
-        sent(t_out + y_out + y_back)
+        sent(t_out[it] + y_out + y_back)
         for copy in gathers + returns:
             copy.wait_send()
 
@@ -673,17 +694,31 @@
             def _(k):
                 spread_copy(k).wait_send()
 
-        sent(t_back)
+        for c, (lo, hi) in enumerate(backs):
+            landed(t_back[c])
+            for j in range(stages):
+                if lo < ROWS * (j + 1) <= hi:
+                    if more:
+                        pack_first(it + 1, j)
+                        y_face(it + 1, j).start()
+                        if j:
+                            run_stage(it + 1, j - 1)
+                    else:
+
+                        def arrived(a, _):
+                            for r in range(ROWS):
+                                x = (a * stages + j) * ROWS + r
+                                set_middle(pot_out, x, pot[ITERS, x])
+                            return 0
+
+                        lax.fori_loop(0, A, arrived, 0)
         if more:
-            x_halo = x_copy(0)
-            for copy in t_halo:
-                copy.wait_send()
-
-            @pl.when(ta == 0)
-            def _():
-                for d in range(A):
-                    x_copy(d).wait_send()
-
+            run_stage(it + 1, stages - 1)
+            for j in range(stages):
+                for d in range(1, A):
+                    t_face(it, j, d).wait_send()
+        unsent = t_back
+    sent(unsent)
     store.wait()
 
 
@@ -699,7 +734,7 @@
 def on_device(sizes, momenta, potential, rho_start, rho_end):
     A, G, B, T, X, Y = sizes
     piece, KT, pieces = X // A, NT // B, G * A
-    stages, groups = piece // ROWS, X // ROWS
+    stages = piece // ROWS
     assert Y == 128 and ROWS * T <= 128 and T % 8 == 0 and piece % ROWS == 0
     assert KT % 8 == 0 and pieces == (KT // 4) * B and ITERS > 1
     table_t, table_y = parts_of(cosine_table(NT)), parts_of(cosine_table(NY))
@@ -723,7 +758,7 @@
     vmem = pl.BlockSpec(memory_space=pltpu.VMEM)
     hbm = pl.BlockSpec(memory_space=pl.ANY)
     dma = pltpu.SemaphoreType.DMA
-    tall = max(groups, 8)
+    chunks = stages + 2
 
     def held(*shape, dtype=f32):
         return pltpu.VMEM(shape, dtype)
@@ -744,15 +779,15 @@
             held(3, NY, NY, dtype=jnp.bfloat16),
             held(3, NY, NY, dtype=jnp.bfloat16),
             held(ITERS + 1, X + 1, T, Y),
-            held(ITERS, X, Y),
-            held(ITERS, tall, Y),
+            held(ITERS, stages, A, 8, Y),
+            held(ITERS, stages, 8, Y),
             held(ITERS, stages, A * ROWS, Y),
             held(ITERS, T, Y),
             held(ITERS, stages, 8, Y),
-            held(ITERS, tall, Y),
+            held(ITERS, stages, 8, Y),
             held(stages, A * ROWS, Y),
             held(stages, 8, Y),
-            held(A, piece, Y),
+            held(stages, A, 8, Y),
             held(X, T, Y),
             held(A, piece, T, Y),
             held(ITERS, piece, NT, Y),
@@ -774,23 +809,27 @@
             held(2, 8, 128),
             held(ITERS, pieces + 1, 8, 128),
             dma((5,)),
-            dma((ITERS, 4)),
-            dma((ITERS, 4)),
+            dma((2,)),
+            dma((2,)),
+            dma((ITERS, stages)),
+            dma((ITERS, stages)),
             dma((ITERS, stages, 2)),
             dma((ITERS, stages, 2)),
-            dma((ITERS, A - 1)),
-            dma((ITERS, A - 1)),
+            dma((ITERS,)),
+            dma((ITERS,)),
+            dma((ITERS, stages, A - 1)),
+            dma((ITERS, stages, A - 1)),
             dma((ITERS, A)),
             dma((ITERS,)),
-            dma((ITERS, 2, stages, A - 1)),
-            dma((ITERS, 2, stages, A - 1)),
-            dma((ITERS, 2, stages, B - 1)),
-            dma((ITERS, 2, stages, B - 1)),
+            dma((ITERS, 2, chunks, A - 1)),
+            dma((ITERS, 2, chunks, A - 1)),
+            dma((ITERS, 2, chunks, B - 1)),
+            dma((ITERS, 2, chunks, B - 1)),
             dma((ITERS, 2, pieces - 1)),
             dma((ITERS, 2, pieces - 1)),
             dma((ITERS, pieces)),
             dma((ITERS, pieces + 1)),
-            dma((ITERS, 4, stages)),
+            dma((ITERS, 4, chunks)),
         ],
         compiler_params=pltpu.CompilerParams(
             collective_id=0, has_side_effects=True, vmem_limit_bytes=60 << 20

time: 205 us -> 196 us (0.956)
  Pallas kernels: 199 us -> 190 us
    pallas_call x1, Pallas kernels: 199 us -> 190 us  [on_device(): pl.pallas_call(functools.partial(kernel, sizes), out_shape=(jax.ShapeDtyp...]
where the time goes in v4:
time: 196 us
  Pallas kernels  190 us (97%)
  local copies, waits for them, and re-layouts  5.03 us (3%)
    pallas_call x1, Pallas kernels, on_device(): pl.pallas_call(functools.partial(kernel, sizes), out_shape=(jax.ShapeDtyp...  190 us
    unnamed x4, local copies, waits for them, and re-layouts  5.03 us

profile of v4, /device:TPU:1, one launch (start us, length us, event | category | flops | bytes accessed | tf_op | source)
XLA Modules:
  0.0 196.0 jit_solution(9336203283045529781)
XLA Ops:
  0.6 190.3 %shard_map.122 = (f32[3,32,64,128]{3,2,1,0:T(8,128)}, f32[32,64,128]{2,1,0:T(8,128)}) custom-call(f32[3,32,64,128]{3,2,1,0:T(8,128)} %mom_hbm.1, f32[32,64,128]{2,1,0:T(8,128)} %pot_in.1, f32[64,128]{1,0:T(8,128)} %rho_start.1, f32[64,128]{1,0:T(8,128)} %rho_end.1, bf16[384,128]{1,0:T(8,128)(2,1)} %constant.14.clone.ct_hbm, ...), custom_call_target="tpu_custom_call" | custom-call | tf_op jit(solution)/shard_map/pallas_call | solution.py:766
  191.0 0.0 copy-start
  191.0 4.1 %copy.15 = f32[3,32,64,128]{3,2,1,0:T(8,128)} copy(f32[3,32,64,128]{3,2,1,0:T(8,128)} %get-tuple-element.4) | data formatting | bytes 6291456
  195.0 0.0 copy-done
  195.0 1.0 copy.16
Async XLA Ops:
  191.0 4.1 %copy-start = (f32[32,64,128]{2,1,0:T(8,128)S(1)}, f32[32,64,128]{2,1,0:T(8,128)}, u32[]{:S(2)}) copy-start(f32[32,64,128]{2,1,0:T(8,128)} %get-tuple-element.5) | copy-start | bytes 3145732

commit v5 on v4

--- a/solution.py
+++ b/solution.py
@@ -14,6 +14,7 @@
 ITERS = 2
 NEWTON = 8
 ROWS = 4
+AHEAD = 4
 
 MESH = pl.DeviceIdType.MESH
 
@@ -43,12 +44,12 @@
     return jnp.dot(left, right, preferred_element_type=jnp.float32)
 
 
-def table_right(value, table):
+def table_right(value, table, kind):
     rows = value.shape[0]
     parts = split(value)
-    total = product(parts[0], table[2])
-    middle_ = product(jnp.concatenate(parts[:2], axis=0), table[1])
-    large = product(jnp.concatenate(parts, axis=0), table[0])
+    total = product(parts[0], table[2, kind])
+    middle_ = product(jnp.concatenate(parts[:2], axis=0), table[1, kind])
+    large = product(jnp.concatenate(parts, axis=0), table[0, kind])
     total = total + (middle_[rows:] + large[2 * rows :])
     total = total + (middle_[:rows] + large[rows : 2 * rows])
     return total + large[:rows]
@@ -57,12 +58,34 @@
 def table_left(table, value):
     rows = table.shape[0] // 3
     parts = split(value)
-    total = product(table[:rows], parts[2])
-    middle_ = product(table[: 2 * rows], parts[1])
-    large = product(table[...], parts[0])
-    total = total + (middle_[rows:] + large[2 * rows :])
-    total = total + (middle_[:rows] + large[rows : 2 * rows])
-    return total + large[:rows]
+    first = product(table[: 2 * rows], jnp.concatenate(parts[:2], axis=0))
+    second = product(table[2 * rows :], jnp.concatenate([parts[2], parts[0]], axis=0))
+    return first[:rows] + (first[rows:] + second)
+
+
+def turned(value):
+    rows, lanes = value.shape
+    index = 127 - lax.broadcasted_iota(jnp.int32, (rows, 128), 1)
+    tiles = [
+        jnp.take_along_axis(value[:, n * 128 : (n + 1) * 128], index, axis=1)
+        for n in range(lanes // 128)
+    ]
+    return jnp.concatenate(tiles[::-1], axis=1)
+
+
+def to_modes(value, table):
+    half = value.shape[1] // 2
+    left, right = value[:, :half], turned(value[:, half:])
+    return jnp.concatenate(
+        [table_right(left + right, table, 0), table_right(left - right, table, 1)], axis=1
+    )
+
+
+def from_modes(value, table):
+    half = value.shape[1] // 2
+    even = table_right(value[:, :half], table, 0)
+    odd = table_right(value[:, half:], table, 1)
+    return jnp.concatenate([even + odd, turned(even - odd)], axis=1)
 
 
 def middle(ref, index):
@@ -391,15 +414,20 @@
             src[0, place(0)] = src[0, place(0)] - jnp.where(gx > 0, hwx[it], 0.0)
             for a in range(1, A):
                 src[a, place(0)] = src[a, place(0)] - wx_all[a * piece - 1]
-        for c, (stage, lo, hi) in enumerate(cuts):
-            if stage == j:
-                t_out[it].append(
-                    along_t(
-                        it, 0, c,
-                        lambda other: src.at[other, pl.ds(lo, hi - lo), :, :],
-                        r1.at[it, pl.ds(lo, hi - lo), pl.ds(ta * T, T), :],
-                    )
+        if j < AHEAD:
+            send_chunk(it)
+
+    def send_chunk(it):
+        c = len(t_out[it])
+        if c < len(cuts):
+            _, lo, hi = cuts[c]
+            t_out[it].append(
+                along_t(
+                    it, 0, c,
+                    lambda other: src.at[other, pl.ds(lo, hi - lo), :, :],
+                    r1.at[it, pl.ds(lo, hi - lo), pl.ds(ta * T, T), :],
                 )
+            )
 
     def run_stage(it, j):
         if it:
@@ -436,6 +464,14 @@
             store.start()
 
         y_out = []
+
+        def forward_y(first_chunk, last_chunk):
+            for c in range(first_chunk, last_chunk + 1):
+                landed(y_out[c])
+            lo, hi = cuts[first_chunk][1], cuts[last_chunk][2]
+            value = r2[it, pl.ds(lo, hi - lo), :, :].reshape((hi - lo) * KT, NY)
+            sp[pl.ds(lo, hi - lo)] = to_modes(value, cyt).reshape(hi - lo, KT, NY)
+
         for c, (_, lo, hi) in enumerate(cuts):
             landed(t_out[it][c])
             for a in range(lo, hi, 2):
@@ -451,18 +487,12 @@
                     r2.at[it, pl.ds(lo, hi - lo), :, pl.ds(pl.multiple_of(gy * Y, Y), Y)],
                 )
             )
-
-        def forward_y(lo, hi):
-            for c in range(len(cuts)):
-                if lo < cuts[c][2] <= hi:
-                    landed(y_out[c])
-            value = r2[it, pl.ds(lo, hi - lo), :, :].reshape((hi - lo) * KT, NY)
-            value = table_right(value, cyt)
-            sp[pl.ds(lo, hi - lo)] = value.reshape(hi - lo, KT, NY)
-
-        bounds = [0, done[max(stages // 2 - 1, 0)], piece - 2, piece]
-        for lo, hi in zip(bounds[:-1], bounds[1:]):
-            forward_y(lo, hi)
+            send_chunk(it)
+            if c == 2:
+                forward_y(0, 1)
+            if c == 3:
+                forward_y(2, 2)
+        forward_y(3, len(cuts) - 1)
 
         def forward(j, _):
             lanes = pl.ds(pl.multiple_of(j * 128, 128), 128)
@@ -616,22 +646,30 @@
                 sq[i, 0:8, 0:128] += jnp.where(constant, excess * ramp + level, 0.0)
 
         y_back, t_back = [], []
-        bounds = [0, 2] + ([backs[2][1]] if stages > 2 else []) + [piece]
-        for lo, hi in zip(bounds[:-1], bounds[1:]):
-            value = table_right(sq[pl.ds(lo, hi - lo)].reshape((hi - lo) * KT, NY), cy)
+
+        def backward_y(first_chunk, last_chunk):
+            lo, hi = backs[first_chunk][0], backs[last_chunk][1]
+            value = from_modes(sq[pl.ds(lo, hi - lo)].reshape((hi - lo) * KT, NY), cy)
             s3[pl.ds(lo, hi - lo)] = value.reshape(hi - lo, KT, NY)
-            for c, (low_row, high_row) in enumerate(backs):
-                if lo <= low_row and high_row <= hi:
-                    lines = pl.ds(low_row, high_row - low_row)
-                    y_back.append(
-                        along_y(
-                            it, 3, c,
-                            lambda other: s3.at[
-                                lines, :, pl.ds(pl.multiple_of(other * Y, Y), Y)
-                            ],
-                            r3.at[it, lines, pl.ds(gy * KT, KT), :],
-                        )
+
+        def send_lines():
+            c = len(y_back)
+            if c < len(backs):
+                lines = pl.ds(backs[c][0], backs[c][1] - backs[c][0])
+                y_back.append(
+                    along_y(
+                        it, 3, c,
+                        lambda other: s3.at[
+                            lines, :, pl.ds(pl.multiple_of(other * Y, Y), Y)
+                        ],
+                        r3.at[it, lines, pl.ds(gy * KT, KT), :],
                     )
+                )
+
+        backward_y(0, 0)
+        send_lines()
+        backward_y(1, 2)
+        send_lines()
         more = it + 1 < ITERS
         sent(unsent)
         if it:
@@ -668,6 +706,9 @@
                     pot.at[it + 1, pl.ds(ta * piece + lo, hi - lo), pl.ds(0, T), :],
                 )
             )
+            send_lines()
+            if c == 0:
+                backward_y(3, len(backs) - 1)
             if more and c == 0:
 
                 @pl.when(ta == 0)
@@ -731,24 +772,34 @@
     return np.stack(parts)
 
 
+def stacked(table):
+    h, m, l = parts_of(table)
+    rows = [[h, h], [m, m], [h, l]]
+    return np.concatenate([np.concatenate(row, axis=1) for row in rows], axis=0)
+
+
 def on_device(sizes, momenta, potential, rho_start, rho_end):
     A, G, B, T, X, Y = sizes
     piece, KT, pieces = X // A, NT // B, G * A
     stages = piece // ROWS
     assert Y == 128 and ROWS * T <= 128 and T % 8 == 0 and piece % ROWS == 0
-    assert KT % 8 == 0 and pieces == (KT // 4) * B and ITERS > 1
-    table_t, table_y = parts_of(cosine_table(NT)), parts_of(cosine_table(NY))
-    turned_t, turned_y = parts_of(cosine_table(NT).T), parts_of(cosine_table(NY).T)
+    assert stages == 4 and KT % 8 == 0 and pieces == (KT // 4) * B and ITERS > 1
+    table_t = stacked(cosine_table(NT))
+    turned_t = stacked(cosine_table(NT).T)
+    folded = cosine_table(NY)[:, : NY // 2].reshape(NY // 2, 2, NY // 2).swapaxes(0, 1)
+    table_y, turned_y = parts_of(folded), parts_of(folded.swapaxes(1, 2))
+    e_y = eigenvalue(NY)
+    e_y = np.concatenate([e_y[0::2], e_y[1::2]])
     e_t = eigenvalue(NT)
     spread_t = np.broadcast_to(e_t[:, None], (NT, 128)).astype(np.float32)
     spread_8 = np.broadcast_to(
         np.concatenate([e_t.reshape(NT // 4, 4)] * 2, axis=1)[:, :, None], (NT // 4, 8, 128)
     ).astype(np.float32)
     spread_y = np.broadcast_to(
-        eigenvalue(NY).reshape(B, 1, 128), (B, 8, 128)
+        e_y.reshape(B, 1, 128), (B, 8, 128)
     ).astype(np.float32)
     tables = [
-        table_t.reshape(3 * NT, NT), turned_t.reshape(3 * NT, NT), table_y, turned_y,
+        table_t, turned_t, table_y, turned_y,
         spread_t, spread_8, spread_y,
     ]
     operands = [momenta, potential, rho_start, rho_end] + [
@@ -774,10 +825,10 @@
         scratch_shapes=[
             held(3, T, X, Y),
             held(3, X, T, Y),
-            held(3 * NT, NT, dtype=jnp.bfloat16),
-            held(3 * NT, NT, dtype=jnp.bfloat16),
-            held(3, NY, NY, dtype=jnp.bfloat16),
-            held(3, NY, NY, dtype=jnp.bfloat16),
+            held(3 * NT, 2 * NT, dtype=jnp.bfloat16),
+            held(3 * NT, 2 * NT, dtype=jnp.bfloat16),
+            held(3, 2, NY // 2, NY // 2, dtype=jnp.bfloat16),
+            held(3, 2, NY // 2, NY // 2, dtype=jnp.bfloat16),
             held(ITERS + 1, X + 1, T, Y),
             held(ITERS, stages, A, 8, Y),
             held(ITERS, stages, 8, Y),

time: 196 us -> 194 us (0.990)
  Pallas kernels: 190 us -> 188 us
where the time goes in v5:
time: 194 us
  Pallas kernels  188 us (97%)
  local copies, waits for them, and re-layouts  5.03 us (3%)
    pallas_call x1, Pallas kernels, on_device(): pl.pallas_call(functools.partial(kernel, sizes), out_shape=(jax.ShapeDtyp...  188 us
    unnamed x4, local copies, waits for them, and re-layouts  5.03 us

profile of v5, /device:TPU:1, one launch (start us, length us, event | category | flops | bytes accessed | tf_op | source)
XLA Modules:
  0.0 194.1 jit_solution(6583849589624062496)
XLA Ops:
  0.6 188.4 %shard_map.122 = (f32[3,32,64,128]{3,2,1,0:T(8,128)}, f32[32,64,128]{2,1,0:T(8,128)}) custom-call(f32[3,32,64,128]{3,2,1,0:T(8,128)} %mom_hbm.1, f32[32,64,128]{2,1,0:T(8,128)} %pot_in.1, f32[64,128]{1,0:T(8,128)} %rho_start.1, f32[64,128]{1,0:T(8,128)} %rho_end.1, bf16[384,256]{1,0:T(8,128)(2,1)} %constant.14.clone.ct_hbm, ...), custom_call_target="tpu_custom_call" | custom-call | tf_op jit(solution)/shard_map/pallas_call | solution.py:817
  189.1 0.0 copy-start
  189.1 4.1 %copy.15 = f32[3,32,64,128]{3,2,1,0:T(8,128)} copy(f32[3,32,64,128]{3,2,1,0:T(8,128)} %get-tuple-element.4) | data formatting | bytes 6291456
  193.1 0.0 copy-done
  193.1 1.0 copy.16
Async XLA Ops:
  189.1 4.1 %copy-start = (f32[32,64,128]{2,1,0:T(8,128)S(1)}, f32[32,64,128]{2,1,0:T(8,128)}, u32[]{:S(2)}) copy-start(f32[32,64,128]{2,1,0:T(8,128)} %get-tuple-element.5) | copy-start | bytes 3145732
